TPU v7x, 128 devices: a whole 4x4x4 slice. The times are simulated.
128 devices in a mesh: grp: 4 (over y), dev: 32 (over x, z, core).
Axes of the slice: x: 4, y: 4, z: 4, core: 2. Of those that a mesh axis runs over, the one named last changes fastest.
Arguments:
- iterate: float32 [216, 131072], P(None, ('grp', 'dev')), may hold values from -6 to 6
- rhs: float32 [216, 131072], P(None, ('grp', 'dev')), may hold values from -12 to 12
- material: float32 [2, 131072], P(None, ('grp', 'dev')), may hold values from 0.25 to 4
- orders: int32 [131072], P(('grp', 'dev')), may hold values from 0 to 4
- new_owner: int32 [131072, 1], P(('grp', 'dev')), may hold values from 0 to 127; in each aligned block of 1024 rows (0 to 1023, 1024 to 2047, ...) at most 16 rows name the same one
- face_send: int32 [2, 65536], P(None, ('grp', 'dev')), may hold values from 0 to 40959
- face_recv: int32 [2, 65536], P(None, ('grp', 'dev')), may hold values from 0 to 40959
- face_flip: int32 [2, 65536], P(None, ('grp', 'dev')), may hold values from 0 to 1
- stiff_off: float32 [5, 216, 216], replicated, may hold values from -0.4375 to 0.4375
- stiff_diag: float32 [5, 216], replicated, may hold values from 1.5 to 3
- mass_diag: float32 [5, 216], replicated, may hold values from 0.25 to 2
Outputs:
- new_iterate: float32 [216, 262144], P(None, ('grp', 'dev'))
- residual: float32 [216, 262144], P(None, ('grp', 'dev'))
Inputs may be any that keep to these rules, and one draw needn't show every extreme that they name: `new_owner`: of one device's 1024 elements at most 16 have the same new owner, and exactly 16 share one for some owner. `face_send`: A row r names dof r // 2048 of slot r % 2048. `face_recv`: A row r names dof r // 2048 of slot r % 2048; rows may repeat.
All inputs are finite; a program needn't handle non-finite values.
Results may differ from a plain program's by a relative error of at most 0.0003.
Values sent between devices are 32-bit elements; how exact they have to be, the bound alone decides.
No kernel may reach another device: no remote copies, remote signals or barrier semaphores. Data moves between devices by JAX's collectives and lax.ppermute only.
A program may use at most 128 MiB of HBM per device.

v0:
```python
import jax
import jax.numpy as jnp
from jax import lax
from jax.sharding import PartitionSpec as P

cheby_weight = 2.0 / (2.0 + 0.2)


def passed_along(array, axis, by):
    devices = lax.axis_size(axis)
    pairs = [(i, i + by) for i in range(devices) if 0 <= i + by < devices]
    return lax.ppermute(array, axis, pairs)


def dof_count(order_index, dof_width):
    order_value = order_index + 2
    return min(dof_width, order_value * (order_value + 2) * (order_value + 3) // 2)


def element_terms(reluctance, mass_coef, order_index, occupied, stiff_diag, mass_diag, dof_width):
    dof_rows = jnp.arange(dof_width, dtype=jnp.int32)[:, None]
    divisor = jnp.ones((dof_width, reluctance.shape[0]), jnp.float32)
    selections = []
    for k in range(stiff_diag.shape[0]):
        selected = (dof_rows < dof_count(k, dof_width)) & ((order_index == k) & occupied)[None, :]
        diag_value = (
            reluctance[None, :] * stiff_diag[k][:, None]
            + mass_coef[None, :] * mass_diag[k][:, None]
        )
        divisor = jnp.where(selected, diag_value, divisor)
        selections.append(selected)
    live_rows = selections[0]
    for selected in selections[1:]:
        live_rows = live_rows | selected
    return (divisor, selections, live_rows)


def apply_block(
    field_dofs, reluctance, mass_coef, order_index, occupied, stiff_off, stiff_diag, mass_diag
):
    dof_width = field_dofs.shape[0]
    divisor, selections, live_rows = element_terms(
        reluctance, mass_coef, order_index, occupied, stiff_diag, mass_diag, dof_width
    )
    summed = jnp.zeros(field_dofs.shape, jnp.float32)
    for k in range(len(selections)):
        masked = jnp.where(selections[k], field_dofs, 0.0)
        product = jnp.dot(
            stiff_off[k],
            masked,
            precision=lax.Precision.HIGHEST,
            preferred_element_type=jnp.float32,
        )
        element_term = (
            reluctance[None, :] * (product + stiff_diag[k][:, None] * masked)
            + mass_coef[None, :] * mass_diag[k][:, None] * masked
        )
        summed = summed + jnp.where(selections[k], element_term, 0.0)
    return (summed, divisor, live_rows)


def per_device(
    iterate,
    rhs,
    material,
    orders,
    new_owner,
    face_send,
    face_recv,
    face_flip,
    stiff_off,
    stiff_diag,
    mass_diag,
):
    dof_width, elem_count = iterate.shape
    owners = lax.axis_size("grp") * lax.axis_size("dev")
    slot_cap = 2 * elem_count // owners
    target = new_owner[:, 0]
    matches = (target[:, None] == jnp.arange(owners, dtype=jnp.int32)[None, :]).astype(jnp.int32)
    earlier = jnp.sum(jnp.cumsum(matches, axis=0) * matches, axis=1) - 1
    slots_at = target * slot_cap + earlier
    coef_local = jnp.concatenate([material, orders.astype(jnp.float32)[None, :]], axis=0)
    stacked = jnp.concatenate([iterate, rhs, coef_local], axis=0)
    stacked_rows = stacked.shape[0]
    packed = jnp.zeros((stacked_rows, owners * slot_cap), jnp.float32).at[:, slots_at].set(stacked)
    arrived = lax.all_to_all(packed, ("grp", "dev"), split_axis=1, concat_axis=1, tiled=True)
    field_dofs = arrived[:dof_width]
    coef_rows = arrived[stacked_rows - 3 :]
    reluctance = coef_rows[0]
    mass_coef = coef_rows[1]
    order_index = coef_rows[2].astype(jnp.int32)
    occupied = reluctance > 0.0
    slot_count = arrived.shape[1]
    source = arrived[dof_width : 2 * dof_width]
    applied, divisor, live_rows = apply_block(
        field_dofs, reluctance, mass_coef, order_index, occupied, stiff_off, stiff_diag, mass_diag
    )
    flat_rows = applied.reshape(-1)
    up_values = flat_rows[face_send[0]]
    down_values = flat_rows[face_send[1]]
    from_below = passed_along(up_values, "dev", 1)
    from_above = passed_along(down_values, "dev", -1)
    face_signs = (1 - 2 * face_flip).astype(jnp.float32)
    flat_rows = flat_rows.at[face_recv[0]].add(face_signs[0] * from_below)
    flat_rows = flat_rows.at[face_recv[1]].add(face_signs[1] * from_above)
    summed = flat_rows.reshape(dof_width, slot_count)
    residual = jnp.where(live_rows, source - summed, 0.0)
    new_iterate = jnp.where(live_rows, field_dofs + cheby_weight * residual / divisor, 0.0)
    return (new_iterate, residual)


def solution(mesh):
    return jax.shard_map(
        per_device,
        mesh=mesh,
        in_specs=(
            P(None, ("grp", "dev")),
            P(None, ("grp", "dev")),
            P(None, ("grp", "dev")),
            P(("grp", "dev")),
            P(("grp", "dev"), None),
            P(None, ("grp", "dev")),
            P(None, ("grp", "dev")),
            P(None, ("grp", "dev")),
            P(),
            P(),
            P(),
        ),
        out_specs=(P(None, ("grp", "dev")), P(None, ("grp", "dev"))),
        check_vma=False,
    )
```

profile of v0, /device:TPU:1, one launch (start us, length us, event | category | flops | bytes accessed | tf_op | source)
XLA Modules:
  0.0 149.6 jit_solution(5008454854151456483)
XLA Ops:
  3.9 1.8 %copy.84 = f32[1024,435]{1,0:T(8,128)} copy(f32[1024,435]{0,1:T(8,128)S(1)} %maximum_bitcast_fusion) | data formatting | bytes 3563520 | tf_op jit(solution)/shard_map/concatenate | solution.py:83
  5.7 7.7 %scatter_custom_fusion = f32[435,2048]{0,1:T(8,128)} fusion(s32[1024]{0:T(1024)S(1)} %bitcast.182, f32[1024,435]{1,0:T(8,128)} %copy.84, f32[]{:T(128)} %constant.18.clone.1), kind=kCustom, calls=%fused_computation.58 | custom fusion | bytes 3564032 | tf_op jit(solution)/shard_map/scatter | solution.py:85
  13.4 12.0 %all-to-all-start = ((f32[435,128,16]{0,2,1:T(8,128)}), f32[435,128,16]{0,2,1:T(8,128)}, u32[]{:S(2)}, u32[]{:S(2)}) async-start(f32[435,128,16]{0,2,1:T(8,128)} %bitcast.144), calls=%async_computation | async-start | bytes 8388608 | tf_op jit(solution)/shard_map/all_to_all | solution.py:86
  27.4 50.6 %all-to-all-done = f32[435,128,16]{0,2,1:T(8,128)} async-done(((f32[435,128,16]{0,2,1:T(8,128)}), f32[435,128,16]{0,2,1:T(8,128)}, u32[]{:S(2)}, u32[]{:S(2)}) %all-to-all-start) | async-done | bytes 3563552 | tf_op jit(solution)/shard_map/all_to_all | solution.py:86
  78.0 3.6 %slice_reduce_fusion.1 = (f32[128,16]{1,0:T(8,128)S(1)}, f32[128,16]{1,0:T(8,128)S(1)}, f32[1,128,16]{0,2,1:T(8,128)S(1)}, f32[1,128,16]{0,2,1:T(8,128)S(1)}) fusion(f32[435,128,16]{0,2,1:T(8,128)} %all-to-all-done), kind=kLoop, calls=%fused_computation.116 | loop fusion | bytes 57344 | tf_op jit(solution)/shard_map/slice | solution.py:89
  84.4 9.1 %and_select_fusion.15 = (f32[216,128,16]{0,2,1:T(8,128)}, f32[216,128,16]{0,2,1:T(8,128)}, f32[216,128,16]{0,2,1:T(8,128)}, f32[216,128,16]{0,2,1:T(8,128)}, f32...) fusion(pred[128,16]{1,0:T(8,128)(4,1)S(1)} %copy.101, ...), kind=kLoop, calls=%fused_computation.60 | loop fusion | flops 4423680 | bytes 15936568 | tf_op jit(solution)/shard_map/jit(_where)/select_n | solution.py:47
  93.5 2.2 %copy.104 = f32[216,2048]{1,0:T(8,128)S(1)} copy(f32[216,2048]{0,1:T(8,128)} %bitcast.147) | data formatting | bytes 3538944 | tf_op jit(solution)/shard_map/slice | solution.py:87
  95.8 4.4 %and_select_fusion.13 = f32[216,2048]{1,0:T(8,128)S(1)} fusion(f32[216,2048]{0,1:T(8,128)} %bitcast.145, f32[216,2048]{1,0:T(8,128)S(1)} %copy.104, f32[216]{0:T(256)S(1)} %bitcast.174, f32[2048]{0:T(1024)S(1)} %mul.123, f32[216]{0:T(256)S(1)} %bitcast.172, f32[2048]{0:T(1024)S(1)} %slice.113, pred[2048]{0:T(1024)(128)(4,1)S(1)} %get-tuple-element.50, ...), kind=kOutput, calls=%fused_computation.22 | convolution fusion | flops 1150599168 | bytes 5550592 | tf_op jit(solution)/shard_map/dot_general | solution.py:48
  100.3 2.8 %fusion.15 = f32[216,2048]{1,0:T(8,128)S(1)} fusion(f32[216,2048]{1,0:T(8,128)S(1)} %and_select_fusion.13, f32[216,2048]{0,1:T(8,128)S(1)} %bitcast.151, f32[216,2048]{1,0:T(8,128)S(1)} %copy.104, f32[216]{0:T(256)S(1)} %bitcast.166, f32[216]{0:T(256)S(1)} %bitcast.158, f32[2048]{0:T(1024)S(1)} %mul.123, f32[2048]{0:T(1024)S(1)} %slice.113, ...), kind=kOutput, calls=%fused_computation.43 | convolution fusion | flops 1151041536 | bytes 7647744 | tf_op jit(solution)/shard_map/dot_general | solution.py:48
  103.2 2.8 %fusion.11 = f32[216,2048]{1,0:T(8,128)S(1)} fusion(f32[216,2048]{1,0:T(8,128)S(1)} %fusion.15, f32[216,2048]{0,1:T(8,128)S(1)} %bitcast.150, f32[216,2048]{1,0:T(8,128)S(1)} %copy.104, f32[216]{0:T(256)S(1)} %bitcast.164, f32[216]{0:T(256)S(1)} %bitcast.156, f32[2048]{0:T(1024)S(1)} %mul.123, f32[2048]{0:T(1024)S(1)} %slice.113, ...), kind=kOutput, calls=%fused_computation.38 | convolution fusion | flops 1151041536 | bytes 7647744 | tf_op jit(solution)/shard_map/dot_general | solution.py:48
  106.1 2.8 %fusion.7 = f32[216,2048]{1,0:T(8,128)S(1)} fusion(f32[216,2048]{1,0:T(8,128)S(1)} %fusion.11, f32[216,2048]{0,1:T(8,128)S(1)} %bitcast.149, f32[216,2048]{1,0:T(8,128)S(1)} %copy.104, f32[216]{0:T(256)S(1)} %bitcast.170, f32[216]{0:T(256)S(1)} %bitcast.162, f32[2048]{0:T(1024)S(1)} %mul.123, f32[2048]{0:T(1024)S(1)} %slice.113, ...), kind=kOutput, calls=%fused_computation.33 | convolution fusion | flops 1151041536 | bytes 7647744 | tf_op jit(solution)/shard_map/dot_general | solution.py:48
  109.0 3.1 %fusion.22 = f32[27,16,8,128]{3,2,1,0:T(8,128)S(1)} fusion(f32[216,2048]{1,0:T(8,128)S(1)} %fusion.7, f32[216,2048]{1,0:T(8,128)S(1)} %copy.104, f32[216,2048]{0,1:T(8,128)S(1)} %bitcast.148, f32[216]{0:T(256)S(1)} %bitcast.168, f32[216]{0:T(256)S(1)} %bitcast.160, f32[2048]{0:T(1024)S(1)} %mul.123, f32[2048]{0:T(1024)S(1)} %slice.113, ...), kind=kOutput, calls=%fused_computation.69 | convolution fusion | flops 1151041536 | bytes 7647744 | tf_op jit(solution)/shard_map/dot_general | solution.py:48
  112.4 4.4 %gather_fusion.1 = f32[512]{0:T(512)} fusion(f32[442368]{0:T(1024)S(1)} %bitcast.141, s32[1024]{0:T(1024)} %pad_clamp_fusion), kind=kCustom, calls=%fused_computation.1 | custom fusion | bytes 6144 | tf_op jit(solution)/shard_map/gather | solution.py:100
  116.9 4.4 %gather_fusion = f32[512]{0:T(512)} fusion(f32[442368]{0:T(1024)S(1)} %bitcast.142, s32[1024]{0:T(1024)} %pad_clamp_fusion.1), kind=kCustom, calls=%fused_computation | custom fusion | bytes 6144 | tf_op jit(solution)/shard_map/gather | solution.py:99
  121.3 3.1 %collective-permute-start = (f32[512]{0:T(512)}, f32[512]{0:T(512)}, u32[]{:S(2)}, u32[]{:S(2)}) collective-permute-start(f32[512]{0:T(512)} %gather_fusion), channel_id=1, source_target_pairs={{0,1},{1,2},{2,3},{3,4},{4,5},{5,6},{6,7},{7,8},{8,9},{9,10},{10,1... | collective-permute-start | bytes 6152 | tf_op jit(solution)/shard_map/ppermute | solution.py:12
  124.4 1.9 %collective-permute-start.1 = (f32[512]{0:T(512)}, f32[512]{0:T(512)}, u32[]{:S(2)}, u32[]{:S(2)}) collective-permute-start(f32[512]{0:T(512)} %gather_fusion.1), channel_id=1, source_target_pairs={{1,0},{2,1},{3,2},{4,3},{5,4},{6,5},{7,6},{8,7},{9,8},{10,9},{11,1... | collective-permute-start | bytes 6152 | tf_op jit(solution)/shard_map/ppermute | solution.py:12
  126.3 1.4 compare_select_fusion.2
  127.7 2.8 %copy.103 = f32[216,2048]{1,0:T(8,128)} copy(f32[216,2048]{0,1:T(8,128)} %bitcast.146) | data formatting | bytes 3538944 | tf_op jit(solution)/shard_map/slice | solution.py:94
  130.5 1.3 mul.322
  131.8 4.1 %scatter_fusion = f32[442368]{0:T(1024)S(1)} fusion(f32[442368]{0:T(1024)S(1)} %bitcast.143, s32[512]{0:T(512)} %bitcast.177, f32[512]{0:T(512)} %mul.322), kind=kCustom, calls=%fused_computation.3 | custom fusion | flops 512 | bytes 8192 | tf_op jit(solution)/shard_map/scatter-add | solution.py:104
  135.9 1.3 mul.323
  137.2 4.1 %scatter_fusion.1 = f32[442368]{0:T(1024)S(1)} fusion(f32[442368]{0:T(1024)S(1)} %scatter_fusion, s32[512]{0:T(512)} %bitcast.176, f32[512]{0:T(512)} %mul.323), kind=kCustom, calls=%fused_computation.4 | custom fusion | flops 512 | bytes 8192 | tf_op jit(solution)/shard_map/scatter-add | solution.py:105
  141.3 1.5 reshape.311
  142.8 6.7 %add_select_fusion = (f32[216,2048]{1,0:T(8,128)}, f32[216,2048]{1,0:T(8,128)}) fusion(f32[216,2048]{1,0:T(8,128)S(1)} %copy.104, f32[216]{0:T(256)} %bitcast.169, f32[216]{0:T(256)} %bitcast.161, f32[216]{0:T(256)} %bitcast.171, f32[216]{0:T(256)} %bitcast.163, f32[216]{0:T(256)} %bitcast.165, f32[216]{0:T(256)} %bitcast.157, f32[216]{0:T(256)} %bitcast.167, ...), kind=kLoop, calls=%fused_computation.67 | loop fusion | flops 15482880 | bytes 8883704 | tf_op jit(solution)/shard_map/jit(_where)/select_n | solution.py:108
  (114 shorter events, 8.2 us)
Async XLA Ops:
  13.4 12.0 %copy-start.29 = (s32[2,512]{1,0:T(2,128)S(1)}, s32[2,512]{1,0:T(2,128)}, u32[]{:S(2)}) copy-start(s32[2,512]{1,0:T(2,128)} %param.16) | copy-start | bytes 12292
  13.4 13.3 %copy-start.30 = (s32[2,512]{1,0:T(2,128)S(1)}, s32[2,512]{1,0:T(2,128)}, u32[]{:S(2)}) copy-start(s32[2,512]{1,0:T(2,128)} %param.18) | copy-start | bytes 12292
  13.4 13.9 %copy-start.31 = (f32[5,216]{1,0:T(8,128)S(1)}, f32[5,216]{1,0:T(8,128)}, u32[]{:S(2)}) copy-start(f32[5,216]{1,0:T(8,128)} %param.20) | copy-start | bytes 12964
  13.4 13.9 %copy-start.32 = (f32[5,216]{1,0:T(8,128)S(1)}, f32[5,216]{1,0:T(8,128)}, u32[]{:S(2)}) copy-start(f32[5,216]{1,0:T(8,128)} %param.21) | copy-start | bytes 12964
  13.4 64.6 %all-to-all-start = ((f32[435,128,16]{0,2,1:T(8,128)}), f32[435,128,16]{0,2,1:T(8,128)}, u32[]{:S(2)}, u32[]{:S(2)}) async-start(f32[435,128,16]{0,2,1:T(8,128)} %bitcast.144), calls=%async_computation | async-start | bytes 8388608 | tf_op jit(solution)/shard_map/all_to_all | solution.py:86
  25.4 70.4 %copy-start.28 = (pred[216]{0:T(512)(128)(4,1)}, pred[216]{0:T(512)(128)(4,1)S(1)}, u32[]{:S(2)}) copy-start(pred[216]{0:T(512)(128)(4,1)S(1)} %iota_compare_fusion.7) | copy-start | bytes 652
  25.4 74.9 %copy-start.25 = (pred[216]{0:T(512)(128)(4,1)}, pred[216]{0:T(512)(128)(4,1)S(1)}, u32[]{:S(2)}) copy-start(pred[216]{0:T(512)(128)(4,1)S(1)} %get-tuple-element.57) | copy-start | bytes 652
  25.4 77.8 %copy-start.24 = (pred[216]{0:T(512)(128)(4,1)}, pred[216]{0:T(512)(128)(4,1)S(1)}, u32[]{:S(2)}) copy-start(pred[216]{0:T(512)(128)(4,1)S(1)} %get-tuple-element.56) | copy-start | bytes 652
  25.4 80.6 %copy-start.27 = (pred[216]{0:T(512)(128)(4,1)}, pred[216]{0:T(512)(128)(4,1)S(1)}, u32[]{:S(2)}) copy-start(pred[216]{0:T(512)(128)(4,1)S(1)} %get-tuple-element.55) | copy-start | bytes 652
  25.4 83.5 %copy-start.26 = (pred[216]{0:T(512)(128)(4,1)}, pred[216]{0:T(512)(128)(4,1)S(1)}, u32[]{:S(2)}) copy-start(pred[216]{0:T(512)(128)(4,1)S(1)} %get-tuple-element.54) | copy-start | bytes 652
  27.3 68.5 %copy-start.21 = (f32[1,216]{1,0:T(1,128)}, f32[1,216]{1,0:T(1,128)S(1)}, u32[]{:S(2)}) copy-start(f32[1,216]{1,0:T(1,128)S(1)} %get-tuple-element.34) | copy-start | bytes 2596
  27.3 73.0 %copy-start.14 = (f32[1,216]{1,0:T(1,128)}, f32[1,216]{1,0:T(1,128)S(1)}, u32[]{:S(2)}) copy-start(f32[1,216]{1,0:T(1,128)S(1)} %get-tuple-element.36) | copy-start | bytes 2596
  27.3 75.9 %copy-start.13 = (f32[1,216]{1,0:T(1,128)}, f32[1,216]{1,0:T(1,128)S(1)}, u32[]{:S(2)}) copy-start(f32[1,216]{1,0:T(1,128)S(1)} %get-tuple-element.35) | copy-start | bytes 2596
  27.3 78.8 %copy-start.16 = (f32[1,216]{1,0:T(1,128)}, f32[1,216]{1,0:T(1,128)S(1)}, u32[]{:S(2)}) copy-start(f32[1,216]{1,0:T(1,128)S(1)} %get-tuple-element.38) | copy-start | bytes 2596
  27.3 81.7 %copy-start.15 = (f32[1,216]{1,0:T(1,128)}, f32[1,216]{1,0:T(1,128)S(1)}, u32[]{:S(2)}) copy-start(f32[1,216]{1,0:T(1,128)S(1)} %get-tuple-element.37) | copy-start | bytes 2596
  27.3 68.4 %copy-start.22 = (f32[1,216]{1,0:T(1,128)}, f32[1,216]{1,0:T(1,128)S(1)}, u32[]{:S(2)}) copy-start(f32[1,216]{1,0:T(1,128)S(1)} %get-tuple-element.39) | copy-start | bytes 2596
  27.4 72.9 %copy-start.18 = (f32[1,216]{1,0:T(1,128)}, f32[1,216]{1,0:T(1,128)S(1)}, u32[]{:S(2)}) copy-start(f32[1,216]{1,0:T(1,128)S(1)} %get-tuple-element.41) | copy-start | bytes 2596
  27.4 75.8 %copy-start.17 = (f32[1,216]{1,0:T(1,128)}, f32[1,216]{1,0:T(1,128)S(1)}, u32[]{:S(2)}) copy-start(f32[1,216]{1,0:T(1,128)S(1)} %get-tuple-element.40) | copy-start | bytes 2596
  27.4 78.7 %copy-start.20 = (f32[1,216]{1,0:T(1,128)}, f32[1,216]{1,0:T(1,128)S(1)}, u32[]{:S(2)}) copy-start(f32[1,216]{1,0:T(1,128)S(1)} %get-tuple-element.43) | copy-start | bytes 2596
  27.4 81.6 %copy-start.19 = (f32[1,216]{1,0:T(1,128)}, f32[1,216]{1,0:T(1,128)S(1)}, u32[]{:S(2)}) copy-start(f32[1,216]{1,0:T(1,128)S(1)} %get-tuple-element.42) | copy-start | bytes 2596
  95.7 13.3 %copy-start.9 = (pred[2048]{0:T(1024)(128)(4,1)}, pred[2048]{0:T(1024)(128)(4,1)S(1)}, u32[]{:S(2)}) copy-start(pred[2048]{0:T(1024)(128)(4,1)S(1)} %get-tuple-element.6) | copy-start | bytes 6148
  95.7 10.4 %copy-start.10 = (pred[2048]{0:T(1024)(128)(4,1)}, pred[2048]{0:T(1024)(128)(4,1)S(1)}, u32[]{:S(2)}) copy-start(pred[2048]{0:T(1024)(128)(4,1)S(1)} %get-tuple-element.51) | copy-start | bytes 6148
  121.3 9.2 %collective-permute-start = (f32[512]{0:T(512)}, f32[512]{0:T(512)}, u32[]{:S(2)}, u32[]{:S(2)}) collective-permute-start(f32[512]{0:T(512)} %gather_fusion), channel_id=1, source_target_pairs={{0,1},{1,2},{2,3},{3,4},{4,5},{5,6},{6,7},{7,8},{8,9},{9,10},{10,1... | collective-permute-start | bytes 6152 | tf_op jit(solution)/shard_map/ppermute | solution.py:12
  124.4 11.5 %collective-permute-start.1 = (f32[512]{0:T(512)}, f32[512]{0:T(512)}, u32[]{:S(2)}, u32[]{:S(2)}) collective-permute-start(f32[512]{0:T(512)} %gather_fusion.1), channel_id=1, source_target_pairs={{1,0},{2,1},{3,2},{4,3},{5,4},{6,5},{7,6},{8,7},{9,8},{10,9},{11,1... | collective-permute-start | bytes 6152 | tf_op jit(solution)/shard_map/ppermute | solution.py:12
  (12 other events, 40.0 us)
where the time goes:
time: 152 us; the launch traced here: 150 us
  waiting for transfers between devices  50.6 us (33%)
  local copies, waits for them, and re-layouts  33.7 us (22%)
  other arithmetic  30.8 us (20%)
  starting transfers between devices  17 us (11%)
  matrix products  16 us (11%)
  between operations  1.53 us (1%)
    all_to_all x1, waiting for transfers between devices, per_device(): lax.all_to_all(packed, ('grp', 'dev'), split_axis=1, concat_axis=1, tiled...  50.6 us
    dot_general x5, matrix products, apply_block(): jnp.dot(stiff_off[k], masked, precision=lax.Precision.HIGHEST, preferred_...  16 us
    all_to_all x1, starting transfers between devices, per_device(): lax.all_to_all(packed, ('grp', 'dev'), split_axis=1, concat_axis=1, tiled...  12 us
    select_n x1, other arithmetic, apply_block(): masked = jnp.where(selections[k], field_dofs, 0.0)  9.07 us
    scatter x1, local copies, waits for them, and re-layouts, per_device(): jnp.zeros((stacked_rows, owners * slot_cap), jnp.float32).at[:, slots_at]  7.7 us
    select_n x1, other arithmetic, per_device(): jnp.where(live_rows, field_dofs + cheby_weight * residual / divisor, 0.0)  6.69 us
    ppermute x2, starting transfers between devices, passed_along(): return lax.ppermute(array, axis, pairs)  5.02 us
    gather x1, local copies, waits for them, and re-layouts, per_device(): down_values = flat_rows[face_send[1]]  4.45 us
  transfers between devices with their start and end apart: 3, of which 1 were waited for; matrix products, arithmetic and copies ran while one was open for 8% of the time, Pallas kernels for 0%

commit v1 on v0

v1 whole, which is shorter than its diff:
```python
import functools

import jax
import jax.numpy as jnp
from jax import lax
from jax.experimental import pallas as pl
from jax.experimental.pallas import tpu as pltpu
from jax.sharding import PartitionSpec as P

F32 = jnp.float32
BF16 = jnp.bfloat16
CHEBY = 2.0 / (2.0 + 0.2)
DOFS = 216
LIVE = (20, 45, 84, 140, 216)
PADDED = (24, 48, 88, 144, 216)
HEAD = 24
BODY = DOFS - HEAD
CAP = 16
ROWS = 56
COEFS = 16
HEAD_ROWS = 8 * HEAD + COEFS
BODY_OFF = sum(n - HEAD for n in PADDED[1:])
BODY_ROWS = BODY_OFF + BODY
NT = (((1,), (1,)), ((), ()))
MIB = 1 << 20


def swapped(array, axis, first):
    devices = lax.axis_size(axis)
    lower = range(first, devices - 1, 2)
    return lax.ppermute(array, axis, [p for i in lower for p in ((i, i + 1), (i + 1, i))])


def two_pieces(x):
    hi = x.astype(BF16)
    return hi, (x - hi.astype(F32)).astype(BF16)


def dot(a, b, dims=(((1,), (0,)), ((), ()))):
    return lax.dot_general(a, b, dims, preferred_element_type=F32)


def coefficients(material, order):
    c0, c1 = material[0:1], material[1:2]
    live = jnp.zeros(order.shape, jnp.int32)
    for k, n in enumerate(LIVE):
        live = jnp.where(order == k, n, live)
    rows = [c0, c1, live.astype(F32), jnp.zeros(order.shape, F32)]
    for c in (c0, c1):
        rows += [jnp.where(order == k, c, 0.0) for k in range(len(LIVE))]
    rows += [jnp.zeros(order.shape, F32)] * (COEFS - len(rows))
    return jnp.concatenate(rows, axis=0)


def ranks_of(own_row, owners):
    chunk = 128
    upper = (
        lax.broadcasted_iota(jnp.int32, (chunk, chunk), 0)
        < lax.broadcasted_iota(jnp.int32, (chunk, chunk), 1)
    )
    sums = jnp.concatenate([upper.astype(F32), jnp.ones((chunk, chunk), F32)], axis=1).astype(BF16)
    carry = jnp.zeros((owners, chunk), F32)
    ranks = []
    for c in range(own_row.shape[1] // chunk):
        named = (
            lax.broadcasted_iota(jnp.int32, (owners, chunk), 0)
            == own_row[:, c * chunk : (c + 1) * chunk]
        ).astype(F32)
        both = dot(named.astype(BF16), sums)
        earlier = both[:, :chunk] + carry
        carry = carry + both[:, chunk:]
        ranks.append(jnp.sum(named * earlier, axis=0, keepdims=True))
    return jnp.concatenate(ranks, axis=1).astype(jnp.int32)


def weights_of(off, diag_t, mass_t):
    lanes = lax.broadcasted_iota(jnp.int32, (DOFS, 256), 1)
    pad = jnp.zeros((DOFS, 256 - DOFS), F32)
    blocks = []
    for k, n in enumerate(LIVE):
        blocks.append(jnp.where(lanes < n, jnp.concatenate([off[k], pad], axis=1), 0.0))
    divisor = jnp.concatenate([jnp.zeros((DOFS, 128), F32), diag_t + mass_t], axis=1)

    def units(rows, start):
        place = lax.broadcasted_iota(jnp.int32, (rows, 256), 0) + start
        return (place == lax.broadcasted_iota(jnp.int32, (rows, 256), 1)).astype(F32)

    head = jnp.concatenate(
        [b[:HEAD] for b in blocks]
        + [divisor[:HEAD], units(HEAD, 0), units(HEAD, DOFS), units(COEFS, 256 - COEFS)],
        axis=0,
    )
    body = jnp.concatenate(
        [b[HEAD:n] for b, n in zip(blocks[1:], PADDED[1:])] + [divisor[HEAD:]], axis=0
    )
    return head, body


def three_passes(w):
    hi, lo = two_pieces(w)
    return jnp.concatenate([hi, lo, hi], axis=1)


def side_by_side(pair, swap):
    both = pair[...]
    there, back = (jnp.concatenate([both[i : i + 1], both[1 - i : 2 - i]], axis=1) for i in (0, 1))
    return jnp.where(swap, back, there)


def odd_device():
    return lax.rem(lax.axis_index("dev"), 2) == 1


def pack_kernel(
    field_in, source_in, material_in, orders_in, owner_in, off_in, diag_in, mass_in, at_in, flip_in,
    out, head_out, body_out, rows_out, lanes_out,
    field, source, material, orders, owner, off, diag, mass, at, flip,
    head_w, body_w, rows_of, lanes_of,
    t0, t1, t2, t3, b0, b1, b2, b3, b4, table, index, placed, in_sems, out_sems, sem,
):
    count = field.shape[1]
    owners = out.shape[0]
    chunk = 128
    loads = []
    for src, dst in (
        (owner_in, owner),
        (field_in, field),
        (source_in, source),
        (orders_in, orders),
        (material_in, material),
        (off_in, off),
        (diag_in, diag),
        (mass_in, mass),
        (at_in, at),
        (flip_in, flip),
    ):
        loads.append(pltpu.make_async_copy(src, dst, in_sems.at[len(loads)]))
        loads[-1].start()
    sends = []

    def send(src, dst):
        sends.append(pltpu.make_async_copy(src, dst, out_sems.at[len(sends)]))
        sends[-1].start()

    b1[...] = jnp.zeros(b1.shape, F32)
    table[...] = jnp.zeros(table.shape, F32)
    loads[0].wait()
    own_row = owner[...]
    index[...] = own_row * CAP + ranks_of(own_row, owners)
    copy = pltpu.make_async_copy(index, placed, sem)
    copy.start()
    for c in loads[1:]:
        c.wait()

    coefs = coefficients(material[...], orders[...])
    for c in range(count // chunk):
        here = slice(c * chunk, (c + 1) * chunk)
        t0[here, :] = field[0:128, here].T
        t1[here, :] = jnp.concatenate(
            [field[128:DOFS, here], source[0:HEAD, here], coefs[:, here]], axis=0
        ).T
        t2[here, :] = source[HEAD : HEAD + 128, here].T
        tail = source[HEAD + 128 : DOFS, here]
        t3[here, :] = jnp.concatenate([tail, tail], axis=0).T

    first = 256 - COEFS + 4 - 128
    orders_held = len(LIVE)
    table[0, first : first + orders_held, 0:DOFS] = diag[...]
    table[1, first + orders_held : first + 2 * orders_held, 0:DOFS] = mass[...]
    head, body = weights_of(off, table[0].T[:DOFS], table[1].T[:DOFS])
    head_w[...] = three_passes(head)
    body_w[...] = three_passes(body)
    swap = jnp.logical_not(odd_device())
    row = side_by_side(at, swap)
    signs = (1 - 2 * side_by_side(flip, swap)).astype(F32)
    faces = row.shape[1]
    mine = lax.broadcasted_iota(jnp.int32, (HEAD * 16, faces), 0) == row // 128
    rows_of[...] = mine.astype(F32).astype(BF16)
    spot = lax.broadcasted_iota(jnp.int32, (128, faces), 0) == lax.rem(row, 128)
    lanes_of[...] = jnp.where(spot, signs, 0.0)
    copy.wait()
    for src, dst in (
        (head_w, head_out),
        (body_w, body_out),
        (rows_of, rows_out),
        (lanes_of, lanes_out),
    ):
        send(src, dst)

    def place(pairs):
        def step(g, carry):
            for j in range(16):
                i = g * 16 + j
                slot = placed[0, i]
                for rows, block in pairs:
                    block[pl.ds(slot, 1), :] = rows[pl.ds(i, 1), :]
            return carry

        lax.fori_loop(0, count // 16, step, 0)

    def send_rows(block, start, size):
        send(block.reshape(owners, size, 128), out.at[:, start : start + size, :])

    place([(t0, b0), (t1, b1)])
    send_rows(b0, 0, CAP)
    send_rows(b1, CAP, CAP)
    place([(t2, b2), (t3, b3)])
    send_rows(b2, 2 * CAP, CAP)
    halves = b3[...].reshape(owners, CAP, 128)
    low = lax.broadcasted_iota(jnp.int32, (owners, CAP // 2, 128), 2) < 64
    b4[...] = jnp.where(low, halves[:, 0 : CAP // 2], halves[:, CAP // 2 :]).reshape(b4.shape)
    send_rows(b4, 3 * CAP, CAP // 2)
    for c in sends:
        c.wait()


def pack(operands, owners):
    count = operands[0].shape[1]
    faces = 2 * operands[-1].shape[1]
    hbm = pl.BlockSpec(memory_space=pltpu.HBM)
    made = [
        jax.ShapeDtypeStruct((HEAD_ROWS, 768), BF16),
        jax.ShapeDtypeStruct((BODY_ROWS, 768), BF16),
        jax.ShapeDtypeStruct((HEAD * 16, faces), BF16),
        jax.ShapeDtypeStruct((128, faces), F32),
    ]
    return pl.pallas_call(
        pack_kernel,
        out_shape=[jax.ShapeDtypeStruct((owners, ROWS, 128), F32)] + made,
        in_specs=[hbm] * len(operands),
        out_specs=[hbm] * 5,
        scratch_shapes=[pltpu.VMEM(a.shape, a.dtype) for a in list(operands) + made]
        + [pltpu.VMEM((count, 128), F32)] * 4
        + [pltpu.VMEM((owners * CAP, 128), F32)] * 4
        + [
            pltpu.VMEM((owners * CAP // 2, 128), F32),
            pltpu.VMEM((2, 128, 256), F32),
            pltpu.VMEM((1, count), jnp.int32),
            pltpu.SMEM((1, count), jnp.int32),
            pltpu.SemaphoreType.DMA((len(operands),)),
            pltpu.SemaphoreType.DMA((8,)),
            pltpu.SemaphoreType.DMA,
        ],
        compiler_params=pltpu.CompilerParams(vmem_limit_bytes=60 * MIB),
        name="pack",
    )(*operands)


def slot_pieces(x0, x1):
    hi, lo = two_pieces(jnp.concatenate([x0, x1], axis=1))
    return jnp.concatenate([hi, hi, lo], axis=1)


def head_kernel(recv, w, send, base, field, step, one, two, applied_at, *, group):
    slots = group * CAP
    for t in range(recv.shape[0] // group):
        at = slice(t * group, (t + 1) * group)
        x0 = recv[at, 0:CAP, :].reshape(-1, 128)
        x1 = recv[at, CAP : 2 * CAP, :].reshape(-1, 128)
        y = dot(w[...], slot_pieces(x0, x1), NT)
        diag, x, rhs = (y[(5 + i) * HEAD : (6 + i) * HEAD] for i in range(3))
        coefs = y[8 * HEAD :]
        c0, live = coefs[0:1], coefs[2:3]
        product = y[0:HEAD]
        for k in range(1, len(LIVE)):
            product = jnp.where(coefs[4 + k : 5 + k] > 0.0, y[k * HEAD : (k + 1) * HEAD], product)
        rows = lax.broadcasted_iota(jnp.int32, (HEAD, slots), 0).astype(F32)
        alive = rows + 0.5 < live
        divisor = jnp.where(alive, diag, 1.0)
        applied = jnp.where(alive, c0 * product + divisor * x, 0.0)
        here = slice(t * slots, (t + 1) * slots)
        applied_at[:, here] = applied
        base[:, here] = jnp.where(alive, rhs - applied, 0.0)
        field[:, here] = jnp.where(alive, x, 0.0)
        step[:, here] = jnp.where(alive, CHEBY / divisor, 0.0)

    row = side_by_side(send, odd_device())
    slot = lax.rem(row, 2048)
    lane, block, dof = lax.rem(slot, 128), slot // 128, row // 2048
    rows = lax.broadcasted_iota(jnp.int32, (8, 128), 0)
    for i in range(row.shape[1] // 128):
        part = slice(i * 128, (i + 1) * 128)
        lanes = jnp.broadcast_to(lane[:, part], (8, 128))
        blocks = jnp.broadcast_to(block[:, part], (8, 128))
        dofs = jnp.broadcast_to(dof[:, part], (8, 128))
        total = jnp.zeros((8, 128), F32)
        for d in range(HEAD // 8):
            found = jnp.zeros((8, 128), F32)
            for b in range(applied_at.shape[1] // 128):
                held = applied_at[d * 8 : (d + 1) * 8, b * 128 : (b + 1) * 128]
                taken = jnp.take_along_axis(held, lanes, axis=1, mode="promise_in_bounds")
                found = jnp.where(blocks == b, taken, found)
            total = total + jnp.where(rows + d * 8 == dofs, found, 0.0)
        values = jnp.sum(total, axis=0, keepdims=True)
        if i < 4:
            one[i : i + 1, :] = values
        else:
            two[i - 4 : i - 3, :] = values


def head_rows(recv, w, face_send, group):
    slots = recv.shape[0] * CAP
    vmem = pl.BlockSpec(memory_space=pltpu.VMEM)
    return pl.pallas_call(
        functools.partial(head_kernel, group=group),
        out_shape=[jax.ShapeDtypeStruct((HEAD, slots), F32)] * 3
        + [jax.ShapeDtypeStruct((4, 128), F32)] * 2,
        in_specs=[vmem] * 3,
        out_specs=[vmem] * 5,
        scratch_shapes=[pltpu.VMEM((HEAD, slots), F32)],
        compiler_params=pltpu.CompilerParams(vmem_limit_bytes=24 * MIB),
        cost_estimate=pl.CostEstimate(flops=2 * 10**9, bytes_accessed=4 * 10**6, transcendentals=0),
        name="head_rows",
    )(recv, w, face_send)


def body_kernel(recv, w, fresh, residual):
    x0, x1, x2 = (recv[:, i * CAP : (i + 1) * CAP, :].reshape(-1, 128) for i in range(3))
    slots = x0.shape[0]
    y = dot(w[...], slot_pieces(x0, x1), NT)
    x1t = x1.T
    field = jnp.concatenate([x0.T[HEAD:], x1t[0 : DOFS - 128]], axis=0)
    last = recv[:, 3 * CAP :, :]
    last = jnp.stack([last, pltpu.roll(last.reshape(-1, 128), 64, 1).reshape(last.shape)], axis=1)
    rhs = jnp.concatenate([x2.T, last.reshape(-1, 128).T[0:64]], axis=0)
    coefs = x1t[128 - COEFS :]
    c0, live = coefs[0:1], coefs[2:3]
    product = None
    start = BODY_OFF
    for k in range(len(LIVE) - 1, 0, -1):
        size = PADDED[k] - HEAD
        start -= size
        mine = y[start : start + size]
        if product is None:
            product = mine
        else:
            top = jnp.where(coefs[4 + k : 5 + k] > 0.0, mine, product[0:size])
            product = jnp.concatenate([top, product[size:]], axis=0)
    rows = lax.broadcasted_iota(jnp.int32, (BODY, slots), 0).astype(F32) + HEAD
    alive = rows + 0.5 < live
    divisor = jnp.where(alive, y[BODY_OFF:], 1.0)
    left = jnp.where(alive, rhs - c0 * product - divisor * field, 0.0)
    residual[HEAD:, :] = left
    fresh[HEAD:, :] = jnp.where(alive, field + CHEBY * left / divisor, 0.0)


def body_rows(recv, w, group):
    partners = recv.shape[0]
    slots = partners * CAP
    wide = pl.BlockSpec((DOFS, group * CAP), lambda t: (0, t))
    return pl.pallas_call(
        body_kernel,
        grid=(partners // group,),
        out_shape=[jax.ShapeDtypeStruct((DOFS, slots), F32)] * 2,
        in_specs=[
            pl.BlockSpec((group, ROWS, 128), lambda t: (t, 0, 0)),
            pl.BlockSpec(memory_space=pltpu.VMEM),
        ],
        out_specs=[wide] * 2,
        compiler_params=pltpu.CompilerParams(vmem_limit_bytes=24 * MIB),
        cost_estimate=pl.CostEstimate(flops=4 * 10**9, bytes_accessed=8 * 10**6, transcendentals=0),
        name="body_rows",
    )(recv, w)


def finish_kernel(one, two, rows_of, lanes_of, base, field, step, _, __, fresh, residual, flat):
    values = jnp.concatenate(
        [one[i : i + 1, :] for i in range(4)] + [two[i : i + 1, :] for i in range(4)], axis=1
    )
    hi, mid = (p.astype(F32) for p in two_pieces(values))
    spread = lanes_of[...]
    pieces = jnp.concatenate([spread * hi, spread * mid, spread * (values - hi - mid)], axis=0)
    found = dot(rows_of[...], pieces.astype(BF16), NT)
    flat[...] = found[:, 0:128] + found[:, 128:256] + found[:, 256:384]
    for b in range(16):
        at = slice(b * 128, (b + 1) * 128)
        added = flat[pl.ds(b, HEAD, stride=16), :]
        scale = step[:, at]
        left = jnp.where(scale > 0.0, base[:, at] - added, 0.0)
        residual[:, at] = left
        fresh[:, at] = field[:, at] + scale * left


def finish(one, two, rows_of, lanes_of, base, field, step, fresh, residual):
    vmem = pl.BlockSpec(memory_space=pltpu.VMEM)
    there = pl.BlockSpec(memory_space=pl.ANY)
    first = pl.BlockSpec(base.shape, lambda t: (0, 0))
    return pl.pallas_call(
        finish_kernel,
        grid=(1,),
        out_shape=[jax.ShapeDtypeStruct(fresh.shape, F32)] * 2,
        in_specs=[vmem] * 7 + [there] * 2,
        out_specs=[first] * 2,
        scratch_shapes=[pltpu.VMEM((HEAD * 16, 128), F32)],
        input_output_aliases={7: 0, 8: 1},
        compiler_params=pltpu.CompilerParams(vmem_limit_bytes=24 * MIB),
        cost_estimate=pl.CostEstimate(flops=10**9, bytes_accessed=10**6, transcendentals=0),
        name="finish",
    )(one, two, rows_of, lanes_of, base, field, step, fresh, residual)


def per_device(
    iterate,
    rhs,
    material,
    orders,
    new_owner,
    face_send,
    face_recv,
    face_flip,
    stiff_off,
    stiff_diag,
    mass_diag,
):
    count = iterate.shape[1]
    owners = lax.axis_size("grp") * lax.axis_size("dev")
    packed, head_w, body_w, rows_of, lanes_of = pack(
        (
            iterate,
            rhs,
            material,
            orders.reshape(1, count),
            new_owner.reshape(1, count),
            stiff_off,
            stiff_diag,
            mass_diag,
            face_recv,
            face_flip,
        ),
        owners,
    )
    recv = lax.all_to_all(packed, ("grp", "dev"), split_axis=0, concat_axis=0, tiled=True)
    base, field, step, one, two = head_rows(recv, head_w, face_send, 16)
    one, two = swapped(one, "dev", 0), swapped(two, "dev", 1)
    fresh, residual = body_rows(recv, body_w, 32)
    return finish(one, two, rows_of, lanes_of, base, field, step, fresh, residual)


def solution(mesh):
    both = ("grp", "dev")
    return jax.shard_map(
        per_device,
        mesh=mesh,
        in_specs=(
            P(None, both),
            P(None, both),
            P(None, both),
            P(both),
            P(both, None),
            P(None, both),
            P(None, both),
            P(None, both),
            P(),
            P(),
            P(),
        ),
        out_specs=(P(None, both), P(None, both)),
        check_vma=False,
    )
```

time: 152 us -> 77.2 us (0.51); the launches traced: 150 us -> 77 us
  blocking collectives: 0 us -> 58.6 us
  waiting for transfers between devices: 50.6 us -> 0.01 us
  local copies, waits for them, and re-layouts: 33.7 us -> 0.02 us
  other arithmetic: 30.8 us -> 0 us
  matrix products: 16 us -> 0 us
  Pallas kernels: 0 us -> 14.2 us
  starting transfers between devices: 17 us -> 3.47 us
    all_to_all x0 -> x1, blocking collectives: none -> 58.6 us  [per_device(): lax.all_to_all(packed, ('grp', 'dev'), split_axis=0, concat_axis=0, tiled...]
    all_to_all x1 -> x0, waiting for transfers between devices: 50.6 us -> none  [per_device(): lax.all_to_all(packed, ('grp', 'dev'), split_axis=1, concat_axis=1, tiled...]
    select_n x5 -> x0, other arithmetic: 17.1 us -> none  [the longest x1 9.07 us: apply_block(): masked = jnp.where(selections[k], field_dofs, 0.0)]
    dot_general x5 -> x0, matrix products: 16 us -> none  [apply_block(): jnp.dot(stiff_off[k], masked, precision=lax.Precision.HIGHEST, preferred_...]
    pallas_call x0 -> x4, Pallas kernels: none -> 14.2 us  [the longest x1 7.02 us: pack(): pl.pallas_call(pack_kernel, out_shape=[jax.ShapeDtypeStruct((owners, ROWS...]
    all_to_all x1 -> x0, starting transfers between devices: 12 us -> none  [per_device(): lax.all_to_all(packed, ('grp', 'dev'), split_axis=1, concat_axis=1, tiled...]
    slice x7 -> x0, local copies, waits for them, and re-layouts: 9.24 us -> none  [the longest x2 3.67 us: per_device(): reluctance = coef_rows[0]]
    gather x2 -> x0, local copies, waits for them, and re-layouts: 8.88 us -> none  [the longest x1 4.45 us: per_device(): down_values = flat_rows[face_send[1]]]
  transfers between devices with their start and end apart: 3 -> 2, of which waited for: 1 -> 0; matrix products, arithmetic and copies ran while one was open for 8% -> 0% of each run, Pallas kernels for 0% -> 6%
where the time goes in v1:
time: 77.2 us; the launch traced here: 77 us
  blocking collectives  58.6 us (76%)
  Pallas kernels  14.2 us (18%)
  starting transfers between devices  3.47 us (4%)
    all_to_all x1, blocking collectives, per_device(): lax.all_to_all(packed, ('grp', 'dev'), split_axis=0, concat_axis=0, tiled...  58.6 us
    pallas_call x1, Pallas kernels, pack(): pl.pallas_call(pack_kernel, out_shape=[jax.ShapeDtypeStruct((owners, ROWS...  7.02 us
    pallas_call x1, Pallas kernels, body_rows(): pl.pallas_call(body_kernel, grid=(partners // group,), out_shape=[jax.Sha...  4.26 us
    ppermute x2, starting transfers between devices, swapped(): lax.ppermute(array, axis, [p for i in lower for p in ((i, i + 1), (i + 1,...  3.47 us
  transfers between devices with their start and end apart: 2, of which 0 were waited for; matrix products, arithmetic and copies ran while one was open for 0% of the time, Pallas kernels for 6%

profile of v1, /device:TPU:1, one launch (start us, length us, event | category | flops | bytes accessed | tf_op | source)
XLA Modules:
  0.0 77.0 jit_solution(17781820777971128453)
XLA Ops:
  0.6 7.0 %pack.1 = (f32[128,56,128]{2,1,0:T(8,128)}, bf16[208,768]{1,0:T(8,128)(2,1)}, bf16[592,768]{1,0:T(8,128)(2,1)}, bf16[384,1024]{1,0:T(8,128)(2,1)}, f32[128,1024]{1,0:T(8,128)}) custom-call(f32[216,1024]{1,0:T(8,128)} %field_in.1, f32[216,1024]{1,0:T(8,128)} %source_in.1, f32[2,1024]{1,0:T(2,128)} %material_in.1, s32[1,1024]{1,0:T(1,128)} %bitcast.2, ...), custom_call_target="tpu_custom_call" | custom-call | tf_op jit(solution)/shard_map/pack/pallas_call | solution.py:227
  7.7 0.0 copy-start.3
  7.7 0.0 copy-start.4
  7.7 58.6 %all_to_all.5.recv = f32[128,56,128]{2,1,0:T(8,128)S(1)} all-to-all(f32[128,56,128]{2,1,0:T(8,128)} %get-tuple-element.14), channel_id=1, replica_groups=mesh['grp'=4,'dev'=32] {'grp','dev'}, dimensions={0} | all-to-all | bytes 7340032 | tf_op jit(solution)/shard_map/all_to_all | solution.py:432
  66.3 0.0 copy-done.3
  66.3 0.0 copy-done.4
  66.3 0.0 copy-start.2
  66.3 1.5 %head_rows.1 = (f32[24,2048]{1,0:T(8,128)S(1)}, f32[24,2048]{1,0:T(8,128)S(1)}, f32[24,2048]{1,0:T(8,128)S(1)}, f32[4,128]{1,0:T(4,128)S(1)}, f32[4,128]{1,0:T(4,128)S(1)}) custom-call(f32[128,56,128]{2,1,0:T(8,128)S(1)} %all_to_all.5.recv, bf16[208,768]{1,0:T(8,128)(2,1)S(1)} %copy-done.3, s32[2,512]{1,0:T(2,128)S(1)} %copy-done.4), custom_call_target="tpu_custom_call" | custom-call | flops 2000000000 | bytes 4000000 | tf_op jit(solution)/shard_map/head_rows/pallas_call | solution.py:304
  67.7 1.4 %collective-permute-start = (f32[4,128]{1,0:T(4,128)S(1)}, f32[4,128]{1,0:T(4,128)S(1)}, u32[]{:S(2)}, u32[]{:S(2)}) collective-permute-start(f32[4,128]{1,0:T(4,128)S(1)} %get-tuple-element.16), channel_id=1, source_target_pairs={{0,1},{1,0},{2,3},{3,2},{4,5},{5,4},{6,7},{7,6},{8,9},{9,8},{10,11... | collective-permute-start | bytes 6152 | tf_op jit(solution)/shard_map/ppermute | solution.py:31
  69.1 2.1 %collective-permute-start.1 = (f32[4,128]{1,0:T(4,128)S(1)}, f32[4,128]{1,0:T(4,128)S(1)}, u32[]{:S(2)}, u32[]{:S(2)}) collective-permute-start(f32[4,128]{1,0:T(4,128)S(1)} %get-tuple-element.17), channel_id=1, source_target_pairs={{1,2},{2,1},{3,4},{4,3},{5,6},{6,5},{7,8},{8,7},{9,10},{10,9},{11,... | collective-permute-start | bytes 6152 | tf_op jit(solution)/shard_map/ppermute | solution.py:31
  71.2 0.0 copy-done.2
  71.2 0.0 copy-start
  71.2 0.0 copy-start.1
  71.3 4.3 %body_rows.1 = (f32[216,2048]{1,0:T(8,128)}, f32[216,2048]{1,0:T(8,128)}) custom-call(f32[128,56,128]{2,1,0:T(8,128)S(1)} %all_to_all.5.recv, bf16[592,768]{1,0:T(8,128)(2,1)S(1)} %copy-done.2), custom_call_target="tpu_custom_call" | custom-call | flops 4000000000 | bytes 8000000 | tf_op jit(solution)/shard_map/body_rows/pallas_call | solution.py:351
  75.5 0.0 collective-permute-done.one
  75.5 0.0 collective-permute-done.1.two
  75.5 0.0 copy-done
  75.5 0.0 copy-done.1
  75.6 1.4 %finish.1 = (f32[216,2048]{1,0:T(8,128)}, f32[216,2048]{1,0:T(8,128)}) custom-call(f32[4,128]{1,0:T(4,128)S(1)} %collective-permute-done.one, f32[4,128]{1,0:T(4,128)S(1)} %collective-permute-done.1.two, bf16[384,1024]{1,0:T(8,128)(2,1)S(1)} %copy-done, f32[128,1024]{1,0:T(8,128)S(1)} %copy-done.1, ...), custom_call_target="tpu_custom_call", output_to_operand_aliasing={{0}: (7, {}), {1}: (8, {})} | custom-call | flops 1000000000 | bytes 1000000 | tf_op jit(solution)/shard_map/finish/pallas_call | solution.py:388
Async XLA Ops:
  7.7 58.6 %copy-start.3 = (bf16[208,768]{1,0:T(8,128)(2,1)S(1)}, bf16[208,768]{1,0:T(8,128)(2,1)}, u32[]{:S(2)}) copy-start(bf16[208,768]{1,0:T(8,128)(2,1)} %get-tuple-element.15.w) | copy-start | bytes 958468
  7.7 58.6 %copy-start.4 = (s32[2,512]{1,0:T(2,128)S(1)}, s32[2,512]{1,0:T(2,128)}, u32[]{:S(2)}) copy-start(s32[2,512]{1,0:T(2,128)} %send.1) | copy-start | bytes 12292
  66.3 5.0 %copy-start.2 = (bf16[592,768]{1,0:T(8,128)(2,1)S(1)}, bf16[592,768]{1,0:T(8,128)(2,1)}, u32[]{:S(2)}) copy-start(bf16[592,768]{1,0:T(8,128)(2,1)} %get-tuple-element.23.w) | copy-start | bytes 2727940
  67.7 7.8 %collective-permute-start = (f32[4,128]{1,0:T(4,128)S(1)}, f32[4,128]{1,0:T(4,128)S(1)}, u32[]{:S(2)}, u32[]{:S(2)}) collective-permute-start(f32[4,128]{1,0:T(4,128)S(1)} %get-tuple-element.16), channel_id=1, source_target_pairs={{0,1},{1,0},{2,3},{3,2},{4,5},{5,4},{6,7},{7,6},{8,9},{9,8},{10,11... | collective-permute-start | bytes 6152 | tf_op jit(solution)/shard_map/ppermute | solution.py:31
  69.1 6.4 %collective-permute-start.1 = (f32[4,128]{1,0:T(4,128)S(1)}, f32[4,128]{1,0:T(4,128)S(1)}, u32[]{:S(2)}, u32[]{:S(2)}) collective-permute-start(f32[4,128]{1,0:T(4,128)S(1)} %get-tuple-element.17), channel_id=1, source_target_pairs={{1,2},{2,1},{3,4},{4,3},{5,6},{6,5},{7,8},{8,7},{9,10},{10,9},{11,... | collective-permute-start | bytes 6152 | tf_op jit(solution)/shard_map/ppermute | solution.py:31
  71.2 4.3 %copy-start = (bf16[384,1024]{1,0:T(8,128)(2,1)S(1)}, bf16[384,1024]{1,0:T(8,128)(2,1)}, u32[]{:S(2)}) copy-start(bf16[384,1024]{1,0:T(8,128)(2,1)} %get-tuple-element.18.rows_of) | copy-start | bytes 2359300
  71.2 4.3 %copy-start.1 = (f32[128,1024]{1,0:T(8,128)S(1)}, f32[128,1024]{1,0:T(8,128)}, u32[]{:S(2)}) copy-start(f32[128,1024]{1,0:T(8,128)} %get-tuple-element.19.lanes_of) | copy-start | bytes 1572868

commit v2 on v1

v2 whole, which is shorter than its diff:
```python
import functools

import jax
import jax.numpy as jnp
from jax import lax
from jax.experimental import pallas as pl
from jax.experimental.pallas import tpu as pltpu
from jax.sharding import PartitionSpec as P

F32 = jnp.float32
BF16 = jnp.bfloat16
CHEBY = 2.0 / (2.0 + 0.2)
DOFS = 216
LIVE = (20, 45, 84, 140, 216)
PADDED = (24, 48, 88, 144, 216)
HEAD = 24
BODY = DOFS - HEAD
CAP = 16
COEFS = 16
NEAR = 88
NEAR_ROWS = CAP + CAP // 2
POOL = 24
POOL_MAX = 2 * CAP
POOL_STRIDE = POOL_MAX + 8
NEAR_W = (len(LIVE) + 3) * HEAD + COEFS
BODY_OFF = sum(n - HEAD for n in PADDED[1:])
BODY_ROWS = BODY_OFF + BODY
NT = (((1,), (1,)), ((), ()))
MIB = 1 << 20


def swapped(array, axis, first):
    devices = lax.axis_size(axis)
    lower = range(first, devices - 1, 2)
    return lax.ppermute(array, axis, [p for i in lower for p in ((i, i + 1), (i + 1, i))])


def two_pieces(x):
    hi = x.astype(BF16)
    return hi, (x - hi.astype(F32)).astype(BF16)


def dot(a, b, dims=(((1,), (0,)), ((), ()))):
    return lax.dot_general(a, b, dims, preferred_element_type=F32)


def coefficients(material, order, first_row, overflow):
    c0, c1 = material[0:1], material[1:2]
    live = jnp.zeros(order.shape, jnp.int32)
    for k, n in enumerate(LIVE):
        live = jnp.where(order == k, n, live)
    rows = [c0, c1, live.astype(F32), first_row]
    for c in (c0, c1):
        rows += [jnp.where(order == k, c, 0.0) for k in range(len(LIVE))]
    rows += [jnp.zeros(order.shape, F32), jnp.broadcast_to(overflow, order.shape)]
    return jnp.concatenate(rows, axis=0)


def ranks_of(own_row, sizes, owners):
    chunk = 128
    upper = (
        lax.broadcasted_iota(jnp.int32, (chunk, chunk), 0)
        < lax.broadcasted_iota(jnp.int32, (chunk, chunk), 1)
    )
    sums = jnp.concatenate([upper.astype(F32), jnp.ones((chunk, chunk), F32)], axis=1).astype(BF16)
    carry = jnp.zeros((2 * owners, chunk), F32)
    ranks, firsts = [], []
    for c in range(own_row.shape[1] // chunk):
        here = slice(c * chunk, (c + 1) * chunk)
        named = (
            lax.broadcasted_iota(jnp.int32, (owners, chunk), 0) == own_row[:, here]
        ).astype(F32)
        marks = jnp.concatenate([named, named * sizes[:, here]], axis=0).astype(BF16)
        both = dot(marks, sums)
        earlier = both[:, :chunk] + carry
        carry = carry + both[:, chunk:]
        ranks.append(jnp.sum(named * earlier[:owners], axis=0, keepdims=True))
        firsts.append(jnp.sum(named * earlier[owners:], axis=0, keepdims=True))
    return (jnp.concatenate(v, axis=1) for v in (ranks, firsts)), jnp.max(carry[owners:])


def weights_of(off, divisor):
    lanes = lax.broadcasted_iota(jnp.int32, (HEAD, 128), 1)

    def units(rows, start):
        place = lax.broadcasted_iota(jnp.int32, (rows, 128), 0) + start
        return (place == lax.broadcasted_iota(jnp.int32, (rows, 128), 1)).astype(F32)

    near = [
        jnp.where(lanes < min(n, NEAR), off[k, 0:HEAD, 0:128], 0.0) for k, n in enumerate(LIVE)
    ]
    near += [pltpu.roll(divisor, 128 - COEFS - (DOFS - 128), 1)[:HEAD]]
    near += [units(HEAD, 0), units(HEAD, NEAR), units(COEFS, 128 - COEFS)]
    pool = [
        jnp.where(lanes < LIVE[k] - NEAR, off[k, 0:HEAD, NEAR:DOFS], 0.0) for k in (4, 3)
    ]
    pad = jnp.zeros((DOFS, 256 - DOFS), F32)
    body = [
        jnp.concatenate([off[k], pad], axis=1)[HEAD:n] for k, n in enumerate(PADDED) if k > 0
    ]
    body += [jnp.concatenate([jnp.zeros((DOFS, 128), F32), divisor], axis=1)[HEAD:]]
    return (jnp.concatenate(v, axis=0) for v in (near, pool, body))


def three_passes(w):
    hi, lo = two_pieces(w)
    return jnp.concatenate([hi, lo, hi], axis=1)


def side_by_side(pair, swap):
    both = pair[...]
    there, back = (jnp.concatenate([both[i : i + 1], both[1 - i : 2 - i]], axis=1) for i in (0, 1))
    return jnp.where(swap, back, there)


def odd_device():
    return lax.rem(lax.axis_index("dev"), 2) == 1


def pack_kernel(
    owner_in, orders_in, at_in, flip_in, material_in, diag_in, mass_in, field_in, source_in, off_in,
    out, extra, near_out, far_out, body_out, rows_out, lanes_out,
    owner, orders, at, flip, material, diag, mass, field, source, off,
    near_w, far_w, body_w, rows_of, lanes_of,
    t0, t1, t2, t3, whole, halves, merged, pool, table,
    slot_index, pool_index, slot_at, pool_at, in_sems, out_sems, index_sems,
):
    count = field.shape[1]
    owners = out.shape[0]
    chunk = 128
    loads = []
    for src, dst in (
        (owner_in, owner),
        (orders_in, orders),
        (at_in, at),
        (flip_in, flip),
        (material_in, material),
        (diag_in, diag),
        (mass_in, mass),
        (field_in, field),
        (source_in, source),
        (off_in, off),
    ):
        loads.append(pltpu.make_async_copy(src, dst, in_sems.at[len(loads)]))
        loads[-1].start()
    sends = []

    def send(src, dst):
        sends.append(pltpu.make_async_copy(src, dst, out_sems.at[len(sends)]))
        sends[-1].start()

    table[...] = jnp.zeros(table.shape, F32)
    for c in loads[0:2]:
        c.wait()
    own_row, order = owner[...], orders[...]
    sizes = jnp.where(order == 4, 2.0, jnp.where(order == 3, 1.0, 0.0))
    (rank, first_row), largest = ranks_of(own_row, sizes, owners)
    slot_index[...] = own_row * CAP + rank.astype(jnp.int32)
    pool_index[...] = own_row * POOL_STRIDE + first_row.astype(jnp.int32)
    copies = [
        pltpu.make_async_copy(src, dst, index_sems.at[i])
        for i, (src, dst) in enumerate(((pool_index, pool_at), (slot_index, slot_at)))
    ]
    for c in copies:
        c.start()
    overflow = jnp.where(largest > POOL, 1.0, 0.0)
    last = lax.broadcasted_iota(jnp.int32, whole.shape, 1) == 127
    whole[...] = jnp.where(last, overflow, 0.0)

    for c in loads[2:7]:
        c.wait()
    swap = jnp.logical_not(odd_device())
    row = side_by_side(at, swap)
    signs = (1 - 2 * side_by_side(flip, swap)).astype(F32)
    faces = row.shape[1]
    mine = lax.broadcasted_iota(jnp.int32, (HEAD * 16, faces), 0) == row // 128
    rows_of[...] = mine.astype(F32).astype(BF16)
    spot = lax.broadcasted_iota(jnp.int32, (128, faces), 0) == lax.rem(row, 128)
    lanes_of[...] = jnp.where(spot, signs, 0.0)
    first = DOFS + 4 - 128
    orders_held = len(LIVE)
    table[first : first + orders_held, 0:DOFS] = diag[...]
    table[first + orders_held : first + 2 * orders_held, 0:DOFS] = mass[...]
    coefs = coefficients(material[...], order, first_row, overflow)

    for c in loads[7:]:
        c.wait()
    for c in range(count // chunk):
        here = slice(c * chunk, (c + 1) * chunk)
        t0[here, :] = jnp.concatenate(
            [field[0:NEAR, here], source[0:HEAD, here], coefs[:, here]], axis=0
        ).T
        middle = source[HEAD:NEAR, here]
        t1[here, :] = jnp.concatenate([middle, middle], axis=0).T
        top = jnp.where(order[:, here] == 4, field[NEAR + 64 : DOFS, here], source[NEAR : NEAR + 64, here])
        t2[here, :] = jnp.concatenate([field[NEAR : NEAR + 64, here], top], axis=0).T
        t3[here, :] = source[NEAR:DOFS, here].T
    near, far, body = weights_of(off, table[...].T[:DOFS])
    near_w[...] = three_passes(near)
    far_w[...] = three_passes(far)
    body_w[...] = three_passes(body)
    for c in copies:
        c.wait()
    for src, dst in (
        (near_w, near_out),
        (far_w, far_out),
        (body_w, body_out),
        (rows_of, rows_out),
        (lanes_of, lanes_out),
    ):
        send(src, dst)

    def place(row_at, steps):
        def step(g, carry):
            for j in range(32):
                i = g * 32 + j
                row = row_at[0, i]
                for rows, block, ahead in steps:
                    block[pl.ds(row + ahead, 1), :] = rows[pl.ds(i, 1), :]
            return carry

        lax.fori_loop(0, count // 32, step, 0)

    place(pool_at, [(t2, pool, 0), (t3, pool, 1)])
    pools = pool.reshape(owners, POOL_STRIDE, 128)
    send(pools.at[:, 0:POOL, :], out.at[:, NEAR_ROWS : NEAR_ROWS + POOL, :])
    send(pools.at[:, POOL:POOL_MAX, :], extra)
    place(slot_at, [(t0, whole, 0), (t1, halves, 0)])
    send(whole.reshape(owners, CAP, 128), out.at[:, 0:CAP, :])
    both = halves[...].reshape(owners, CAP, 128)
    low = lax.broadcasted_iota(jnp.int32, (owners, CAP // 2, 128), 2) < 64
    both = jnp.where(low, both[:, 0 : CAP // 2], both[:, CAP // 2 :])
    merged[...] = both.reshape(merged.shape)
    send(merged.reshape(owners, CAP // 2, 128), out.at[:, CAP:NEAR_ROWS, :])
    for c in sends:
        c.wait()


def pack(operands, owners):
    count = operands[0].shape[1]
    faces = 2 * operands[2].shape[1]
    hbm = pl.BlockSpec(memory_space=pltpu.HBM)
    made = [
        jax.ShapeDtypeStruct((NEAR_W, 384), BF16),
        jax.ShapeDtypeStruct((2 * HEAD, 384), BF16),
        jax.ShapeDtypeStruct((BODY_ROWS, 768), BF16),
        jax.ShapeDtypeStruct((HEAD * 16, faces), BF16),
        jax.ShapeDtypeStruct((128, faces), F32),
    ]
    return pl.pallas_call(
        pack_kernel,
        out_shape=[
            jax.ShapeDtypeStruct((owners, NEAR_ROWS + POOL, 128), F32),
            jax.ShapeDtypeStruct((owners, POOL_MAX - POOL, 128), F32),
        ]
        + made,
        in_specs=[hbm] * len(operands),
        out_specs=[hbm] * 7,
        scratch_shapes=[pltpu.VMEM(a.shape, a.dtype) for a in list(operands) + made]
        + [pltpu.VMEM((count, 128), F32)] * 4
        + [pltpu.VMEM((owners * CAP, 128), F32)] * 2
        + [
            pltpu.VMEM((owners * CAP // 2, 128), F32),
            pltpu.VMEM((owners * POOL_STRIDE, 128), F32),
            pltpu.VMEM((128, 256), F32),
            pltpu.VMEM((1, count), jnp.int32),
            pltpu.VMEM((1, count), jnp.int32),
            pltpu.SMEM((1, count), jnp.int32),
            pltpu.SMEM((1, count), jnp.int32),
            pltpu.SemaphoreType.DMA((len(operands),)),
            pltpu.SemaphoreType.DMA((9,)),
            pltpu.SemaphoreType.DMA((2,)),
        ],
        compiler_params=pltpu.CompilerParams(vmem_limit_bytes=60 * MIB),
        name="pack",
    )(*operands)


def pool_columns(pools, first_row):
    rows, wide = pools.shape
    partners = first_row.shape[1] // CAP
    held = wide // partners
    lane = lax.broadcasted_iota(jnp.int32, (1, 128), 1)
    tiles = []
    for j in range(partners // 8):
        start = j * 8 * held
        tile = start // 128
        at = start % 128 + lane // CAP * held + first_row[:, j * 128 : (j + 1) * 128]
        second = jnp.broadcast_to(at >= 128, (8, 128))
        at = jnp.broadcast_to(jnp.bitwise_and(at, 127), (8, 128))

        def taken(r, tile):
            part = pools[r : r + 8, tile * 128 : (tile + 1) * 128]
            return jnp.take_along_axis(part, at, axis=1, mode="promise_in_bounds")

        tiles.append(
            jnp.concatenate(
                [jnp.where(second, taken(r, tile + 1), taken(r, tile)) for r in range(0, rows, 8)],
                axis=0,
            )
        )
    return jnp.concatenate(tiles, axis=1)


def field_pieces(values):
    wide = values.shape[1]
    full = jnp.concatenate([values, jnp.zeros((256 - values.shape[0], wide), F32)], axis=0)
    hi, lo = two_pieces(full)
    return jnp.concatenate([hi, hi, lo], axis=0)


def flag_kernel(recv, flag, same):
    flags = jnp.max(jnp.max(recv[:, 0:8, :], axis=0), axis=0, keepdims=True)
    last = lax.broadcasted_iota(jnp.int32, flags.shape, 1) == 127
    flag[...] = jnp.max(jnp.where(last, flags, 0.0), axis=1, keepdims=True)
    same[...] = flag[...]


def flag_of(recv):
    vmem = pl.BlockSpec(memory_space=pltpu.VMEM)
    return pl.pallas_call(
        flag_kernel,
        out_shape=[jax.ShapeDtypeStruct((1, 1), F32)] * 2,
        in_specs=[vmem],
        out_specs=[vmem] * 2,
        compiler_params=pltpu.CompilerParams(vmem_limit_bytes=16 * MIB),
        name="flag_of",
    )(recv)


def load_overflow(flag, extra, more, sem):
    @pl.when(jnp.max(flag[...]) > 0.5)
    def _():
        copy = pltpu.make_async_copy(extra, more, sem)
        copy.start()
        copy.wait()


def row_pieces(rows):
    hi, lo = two_pieces(rows)
    return jnp.concatenate([hi, hi, lo], axis=1)


def head_kernel(
    recv, flag, extra, near_w, far_w, send,
    base, field, step, one, two, applied_at, more, sem, *, group,
):
    load_overflow(flag, extra, more, sem)
    slots = group * CAP
    for t in range(recv.shape[0] // group):
        at = slice(t * group, (t + 1) * group)
        here = slice(t * slots, (t + 1) * slots)
        near = recv[at, 0:CAP, :].reshape(-1, 128)
        pools = jnp.concatenate([recv[at, NEAR_ROWS:, :], more[at]], axis=1).reshape(-1, 128)
        y = dot(near_w[...], row_pieces(near), NT)
        z = dot(far_w[...], row_pieces(pools), NT)
        diag, x, rhs = (y[(5 + i) * HEAD : (6 + i) * HEAD] for i in range(3))
        coefs = y[8 * HEAD :]
        c0, live = coefs[0:1], coefs[2:3]
        far = pool_columns(z, (coefs[3:4] + 0.5).astype(jnp.int32))
        product = y[0:HEAD]
        for k in range(1, len(LIVE)):
            mine = y[k * HEAD : (k + 1) * HEAD]
            if k >= 3:
                mine = mine + far[(4 - k) * HEAD : (5 - k) * HEAD]
            product = jnp.where(coefs[4 + k : 5 + k] > 0.0, mine, product)
        rows = lax.broadcasted_iota(jnp.int32, (HEAD, slots), 0).astype(F32)
        alive = rows + 0.5 < live
        divisor = jnp.where(alive, diag, 1.0)
        applied = jnp.where(alive, c0 * product + divisor * x, 0.0)
        applied_at[:, here] = applied
        base[:, here] = jnp.where(alive, rhs - applied, 0.0)
        field[:, here] = jnp.where(alive, x, 0.0)
        step[:, here] = jnp.where(alive, CHEBY / divisor, 0.0)

    row = side_by_side(send, odd_device())
    slot = lax.rem(row, 2048)
    lane, block, dof = lax.rem(slot, 128), slot // 128, row // 2048
    rows = lax.broadcasted_iota(jnp.int32, (8, 128), 0)
    for i in range(row.shape[1] // 128):
        part = slice(i * 128, (i + 1) * 128)
        lanes = jnp.broadcast_to(lane[:, part], (8, 128))
        blocks = jnp.broadcast_to(block[:, part], (8, 128))
        dofs = jnp.broadcast_to(dof[:, part], (8, 128))
        total = jnp.zeros((8, 128), F32)
        for d in range(HEAD // 8):
            found = jnp.zeros((8, 128), F32)
            for b in range(applied_at.shape[1] // 128):
                held = applied_at[d * 8 : (d + 1) * 8, b * 128 : (b + 1) * 128]
                taken = jnp.take_along_axis(held, lanes, axis=1, mode="promise_in_bounds")
                found = jnp.where(blocks == b, taken, found)
            total = total + jnp.where(rows + d * 8 == dofs, found, 0.0)
        values = jnp.sum(total, axis=0, keepdims=True)
        if i < 4:
            one[i : i + 1, :] = values
        else:
            two[i - 4 : i - 3, :] = values


def head_rows(recv, flag, extra, near_w, far_w, face_send, group):
    slots = recv.shape[0] * CAP
    vmem = pl.BlockSpec(memory_space=pltpu.VMEM)
    there = pl.BlockSpec(memory_space=pltpu.HBM)
    return pl.pallas_call(
        functools.partial(head_kernel, group=group),
        out_shape=[jax.ShapeDtypeStruct((HEAD, slots), F32)] * 3
        + [jax.ShapeDtypeStruct((4, 128), F32)] * 2,
        in_specs=[vmem] * 2 + [there] + [vmem] * 3,
        out_specs=[vmem] * 5,
        scratch_shapes=[
            pltpu.VMEM((HEAD, slots), F32),
            pltpu.VMEM(extra.shape, F32),
            pltpu.SemaphoreType.DMA,
        ],
        compiler_params=pltpu.CompilerParams(vmem_limit_bytes=24 * MIB),
        cost_estimate=pl.CostEstimate(flops=2 * 10**9, bytes_accessed=4 * 10**6, transcendentals=0),
        name="head_rows",
    )(recv, flag, extra, near_w, far_w, face_send)


def body_kernel(recv, flag, extra, w, fresh, residual, more, sem):
    t = pl.program_id(0)

    @pl.when(t == 0)
    def _():
        load_overflow(flag, extra, more, sem)

    group = recv.shape[0]
    slots = group * CAP
    near = recv[:, 0:CAP, :].reshape(-1, 128).T
    middle = recv[:, CAP:NEAR_ROWS, :]
    turned = pltpu.roll(middle.reshape(-1, 128), 64, 1).reshape(middle.shape)
    middle = jnp.stack([middle, turned], axis=1).reshape(-1, 128).T[0:64]
    rest = more[pl.ds(t * group, group), :, :]
    pools = jnp.concatenate([recv[:, NEAR_ROWS:, :], rest], axis=1).reshape(-1, 128).T
    coefs = near[128 - COEFS :]
    c0, live = coefs[0:1], coefs[2:3]
    first_row = coefs[3:4].astype(jnp.int32)
    far = pool_columns(pools, first_row)
    far_rhs = pool_columns(pools, first_row + 1)
    rows = lax.broadcasted_iota(jnp.int32, (DOFS, slots), 0).astype(F32)
    alive = rows + 0.5 < live
    values = jnp.where(alive, jnp.concatenate([near[0:NEAR], far], axis=0), 0.0)
    y = dot(w[...], field_pieces(jnp.concatenate([values, coefs], axis=0)))
    top = jnp.where(coefs[8:9] > 0.0, far_rhs[0:64], far[64:128])
    rhs = jnp.concatenate([middle, top, far_rhs[64:]], axis=0)
    product = None
    start = BODY_OFF
    for k in range(len(LIVE) - 1, 0, -1):
        size = PADDED[k] - HEAD
        start -= size
        mine = y[start : start + size]
        if product is None:
            product = mine
        else:
            best = jnp.where(coefs[4 + k : 5 + k] > 0.0, mine, product[0:size])
            product = jnp.concatenate([best, product[size:]], axis=0)
    alive = alive[HEAD:]
    field = values[HEAD:]
    divisor = jnp.where(alive, y[BODY_OFF:], 1.0)
    left = jnp.where(alive, rhs - c0 * product - divisor * field, 0.0)
    residual[HEAD:, :] = left
    fresh[HEAD:, :] = field + CHEBY * left / divisor


def body_rows(recv, flag, extra, w, group):
    partners, rows = recv.shape[:2]
    slots = partners * CAP
    vmem = pl.BlockSpec(memory_space=pltpu.VMEM)
    wide = pl.BlockSpec((DOFS, group * CAP), lambda t: (0, t))
    return pl.pallas_call(
        body_kernel,
        grid=(partners // group,),
        out_shape=[jax.ShapeDtypeStruct((DOFS, slots), F32)] * 2,
        in_specs=[
            pl.BlockSpec((group, rows, 128), lambda t: (t, 0, 0)),
            vmem,
            pl.BlockSpec(memory_space=pltpu.HBM),
            vmem,
        ],
        out_specs=[wide] * 2,
        scratch_shapes=[pltpu.VMEM(extra.shape, F32), pltpu.SemaphoreType.DMA],
        compiler_params=pltpu.CompilerParams(vmem_limit_bytes=24 * MIB),
        cost_estimate=pl.CostEstimate(flops=4 * 10**9, bytes_accessed=8 * 10**6, transcendentals=0),
        name="body_rows",
    )(recv, flag, extra, w)


def finish_kernel(one, two, rows_of, lanes_of, base, field, step, _, __, fresh, residual, flat):
    values = jnp.concatenate(
        [one[i : i + 1, :] for i in range(4)] + [two[i : i + 1, :] for i in range(4)], axis=1
    )
    hi, mid = (p.astype(F32) for p in two_pieces(values))
    spread = lanes_of[...]
    pieces = jnp.concatenate([spread * hi, spread * mid, spread * (values - hi - mid)], axis=0)
    found = dot(rows_of[...], pieces.astype(BF16), NT)
    flat[...] = found[:, 0:128] + found[:, 128:256] + found[:, 256:384]
    for b in range(16):
        at = slice(b * 128, (b + 1) * 128)
        added = flat[pl.ds(b, HEAD, stride=16), :]
        scale = step[:, at]
        left = jnp.where(scale > 0.0, base[:, at] - added, 0.0)
        residual[:, at] = left
        fresh[:, at] = field[:, at] + scale * left


def finish(one, two, rows_of, lanes_of, base, field, step, fresh, residual):
    vmem = pl.BlockSpec(memory_space=pltpu.VMEM)
    there = pl.BlockSpec(memory_space=pl.ANY)
    first = pl.BlockSpec(base.shape, lambda t: (0, 0))
    return pl.pallas_call(
        finish_kernel,
        grid=(1,),
        out_shape=[jax.ShapeDtypeStruct(fresh.shape, F32)] * 2,
        in_specs=[vmem] * 7 + [there] * 2,
        out_specs=[first] * 2,
        scratch_shapes=[pltpu.VMEM((HEAD * 16, 128), F32)],
        input_output_aliases={7: 0, 8: 1},
        compiler_params=pltpu.CompilerParams(vmem_limit_bytes=24 * MIB),
        cost_estimate=pl.CostEstimate(flops=10**9, bytes_accessed=10**6, transcendentals=0),
        name="finish",
    )(one, two, rows_of, lanes_of, base, field, step, fresh, residual)


def per_device(
    iterate,
    rhs,
    material,
    orders,
    new_owner,
    face_send,
    face_recv,
    face_flip,
    stiff_off,
    stiff_diag,
    mass_diag,
):
    count = iterate.shape[1]
    owners = lax.axis_size("grp") * lax.axis_size("dev")
    packed, extra, near_w, far_w, body_w, rows_of, lanes_of = pack(
        (
            new_owner.reshape(1, count),
            orders.reshape(1, count),
            face_recv,
            face_flip,
            material,
            stiff_diag,
            mass_diag,
            iterate,
            rhs,
            stiff_off,
        ),
        owners,
    )

    def exchanged(rows):
        return lax.all_to_all(rows, ("grp", "dev"), split_axis=0, concat_axis=0, tiled=True)

    recv = exchanged(packed)
    flag, same = flag_of(recv)
    _, extra = lax.while_loop(
        lambda c: c[0] > 0.5,
        lambda c: (jnp.zeros((), F32), exchanged(c[1])),
        (flag[0, 0], extra),
    )
    base, field, step, one, two = head_rows(recv, same, extra, near_w, far_w, face_send, 16)
    one, two = swapped(one, "dev", 0), swapped(two, "dev", 1)
    fresh, residual = body_rows(recv, same, extra, body_w, 32)
    return tuple(finish(one, two, rows_of, lanes_of, base, field, step, fresh, residual))


def solution(mesh):
    both = ("grp", "dev")
    return jax.shard_map(
        per_device,
        mesh=mesh,
        in_specs=(
            P(None, both),
            P(None, both),
            P(None, both),
            P(both),
            P(both, None),
            P(None, both),
            P(None, both),
            P(None, both),
            P(),
            P(),
            P(),
        ),
        out_specs=(P(None, both), P(None, both)),
        check_vma=False,
    )
```

time: 77.2 us -> 76.7 us (level)
  blocking collectives: 58.6 us -> 52.9 us
  Pallas kernels: 14.2 us -> 18.5 us
    all_to_all x1, blocking collectives: 58.6 us -> 52.9 us  [exchanged(): lax.all_to_all(rows, ('grp', 'dev'), split_axis=0, concat_axis=0, tiled=T...]
    pallas_call x1, Pallas kernels: 4.26 us -> 7.21 us  [body_rows(): pl.pallas_call(body_kernel, grid=(partners // group,), out_shape=[jax.Sha...]
    pallas_call x1, Pallas kernels: 1.48 us -> 2.74 us  [head_rows(): pl.pallas_call(functools.partial(head_kernel, group=group), out_shape=[ja...]
    pallas_call x1 -> x2, Pallas kernels: 7.02 us -> 7.14 us  [the longest x1 6.35 us: pack(): pl.pallas_call(pack_kernel, out_shape=[jax.ShapeDtypeStruct((owners, NEAR...]
  transfers between devices with their start and end apart: 2 -> 2, of which waited for: 0 -> 0; matrix products, arithmetic and copies ran while one was open for 0% -> 0% of each run, Pallas kernels for 6% -> 9%
where the time goes in v2:
time: 76.7 us; the launch traced here: 76.4 us
  blocking collectives  52.9 us (69%)
  Pallas kernels  18.5 us (24%)
  starting transfers between devices  3.3 us (4%)
    all_to_all x1, blocking collectives, exchanged(): lax.all_to_all(rows, ('grp', 'dev'), split_axis=0, concat_axis=0, tiled=T...  52.9 us
    pallas_call x1, Pallas kernels, body_rows(): pl.pallas_call(body_kernel, grid=(partners // group,), out_shape=[jax.Sha...  7.21 us
    pallas_call x1, Pallas kernels, pack(): pl.pallas_call(pack_kernel, out_shape=[jax.ShapeDtypeStruct((owners, NEAR...  6.35 us
    ppermute x2, starting transfers between devices, swapped(): lax.ppermute(array, axis, [p for i in lower for p in ((i, i + 1), (i + 1,...  3.3 us
    pallas_call x1, Pallas kernels, head_rows(): pl.pallas_call(functools.partial(head_kernel, group=group), out_shape=[ja...  2.74 us
  transfers between devices with their start and end apart: 2, of which 0 were waited for; matrix products, arithmetic and copies ran while one was open for 0% of the time, Pallas kernels for 9%

profile of v2, /device:TPU:1, one launch (start us, length us, event | category | flops | bytes accessed | tf_op | source)
XLA Modules:
  0.0 76.4 jit_solution(4581909500282500807)
XLA Ops:
  0.6 6.3 %pack.1 = (f32[128,48,128]{2,1,0:T(8,128)}, f32[128,8,128]{2,1,0:T(8,128)}, bf16[208,384]{1,0:T(8,128)(2,1)}, bf16[48,384]{1,0:T(8,128)(2,1)}, bf16[592,768]{1,0...) custom-call(s32[1,1024]{1,0:T(1,128)} %bitcast.3, s32[1,1024]{1,0:T(1,128)} %bitcast.4, s32[2,512]{1,0:T(2,128)} %at_in.1, ...), custom_call_target="tpu_custom_call" | custom-call | tf_op jit(solution)/shard_map/pack/pallas_call | solution.py:250
  7.0 52.9 %all_to_all.9.recv = f32[128,48,128]{2,1,0:T(8,128)S(1)} all-to-all(f32[128,48,128]{2,1,0:T(8,128)} %get-tuple-element.29), channel_id=1, replica_groups=mesh['grp'=4,'dev'=32] {'grp','dev'}, dimensions={0} | all-to-all | bytes 6291456 | tf_op jit(solution)/shard_map/all_to_all | solution.py:557
  59.9 0.8 %flag_of.1 = (f32[1,1]{1,0:T(1,128)}, f32[1,1]{1,0:T(1,128)}) custom-call(f32[128,48,128]{2,1,0:T(8,128)S(1)} %all_to_all.9.recv), custom_call_target="tpu_custom_call" | custom-call | tf_op jit(solution)/shard_map/flag_of/pallas_call | solution.py:321
  60.7 0.0 copy-start.3
  60.7 0.0 copy-start.4
  60.7 0.0 copy-start.5
  60.7 0.6 while.9
  61.3 0.3 copy-done.3
  61.6 0.0 copy-done.4
  61.6 0.0 copy-done.5
  61.6 0.0 copy-start.2
  61.6 2.7 %head_rows.1 = (f32[24,2048]{1,0:T(8,128)S(1)}, f32[24,2048]{1,0:T(8,128)S(1)}, f32[24,2048]{1,0:T(8,128)S(1)}, f32[4,128]{1,0:T(4,128)S(1)}, f32[4,128]{1,0:T(4,128)S(1)}) custom-call(f32[128,48,128]{2,1,0:T(8,128)S(1)} %all_to_all.9.recv, f32[1,1]{1,0:T(1,128)} %get-tuple-element.30.flag, f32[128,8,128]{2,1,0:T(8,128)} %get-tuple-element.33.extra, ...), custom_call_target="tpu_custom_call" | custom-call | flops 2000000000 | bytes 4000000 | tf_op jit(solution)/shard_map/head_rows/pallas_call | solution.py:404
  64.4 1.4 %collective-permute-start = (f32[4,128]{1,0:T(4,128)S(1)}, f32[4,128]{1,0:T(4,128)S(1)}, u32[]{:S(2)}, u32[]{:S(2)}) collective-permute-start(f32[4,128]{1,0:T(4,128)S(1)} %get-tuple-element.36), channel_id=1, source_target_pairs={{0,1},{1,0},{2,3},{3,2},{4,5},{5,4},{6,7},{7,6},{8,9},{9,8},{10,11... | collective-permute-start | bytes 6152 | tf_op jit(solution)/shard_map/ppermute | solution.py:35
  65.8 1.9 %collective-permute-start.1 = (f32[4,128]{1,0:T(4,128)S(1)}, f32[4,128]{1,0:T(4,128)S(1)}, u32[]{:S(2)}, u32[]{:S(2)}) collective-permute-start(f32[4,128]{1,0:T(4,128)S(1)} %get-tuple-element.37), channel_id=1, source_target_pairs={{1,2},{2,1},{3,4},{4,3},{5,6},{6,5},{7,8},{8,7},{9,10},{10,9},{11,... | collective-permute-start | bytes 6152 | tf_op jit(solution)/shard_map/ppermute | solution.py:35
  67.7 0.0 copy-done.2
  67.7 0.0 copy-done.6
  67.7 0.0 copy-start
  67.7 0.0 copy-start.1
  67.7 7.2 %body_rows.1 = (f32[216,2048]{1,0:T(8,128)}, f32[216,2048]{1,0:T(8,128)}) custom-call(f32[128,48,128]{2,1,0:T(8,128)S(1)} %all_to_all.9.recv, f32[1,1]{1,0:T(1,128)} %get-tuple-element.30.flag, f32[128,8,128]{2,1,0:T(8,128)S(1)} %copy-done.6, bf16[592,768]{1,0:T(8,128)(2,1)S(1)} %copy-done.2), custom_call_target="tpu_custom_call" | custom-call | flops 4000000000 | bytes 8000000 | tf_op jit(solution)/shard_map/body_rows/pallas_call | solution.py:471
  75.0 0.0 collective-permute-done.one
  75.0 0.0 collective-permute-done.1.two
  75.0 0.0 copy-done
  75.0 0.0 copy-done.1
  75.0 1.4 %finish.1 = (f32[216,2048]{1,0:T(8,128)}, f32[216,2048]{1,0:T(8,128)}) custom-call(f32[4,128]{1,0:T(4,128)S(1)} %collective-permute-done.one, f32[4,128]{1,0:T(4,128)S(1)} %collective-permute-done.1.two, bf16[384,1024]{1,0:T(8,128)(2,1)S(1)} %copy-done, f32[128,1024]{1,0:T(8,128)S(1)} %copy-done.1, ...), custom_call_target="tpu_custom_call", output_to_operand_aliasing={{0}: (7, {}), {1}: (8, {})} | custom-call | flops 1000000000 | bytes 1000000 | tf_op jit(solution)/shard_map/finish/pallas_call | solution.py:511
  (1 shorter events, 0.0 us)
Async XLA Ops:
  60.7 0.9 %copy-start.3 = (bf16[208,384]{1,0:T(8,128)(2,1)S(1)}, bf16[208,384]{1,0:T(8,128)(2,1)}, u32[]{:S(2)}) copy-start(bf16[208,384]{1,0:T(8,128)(2,1)} %get-tuple-element.34.near_w) | copy-start | bytes 479236
  60.7 0.9 %copy-start.4 = (bf16[48,384]{1,0:T(8,128)(2,1)S(1)}, bf16[48,384]{1,0:T(8,128)(2,1)}, u32[]{:S(2)}) copy-start(bf16[48,384]{1,0:T(8,128)(2,1)} %get-tuple-element.35.far_w) | copy-start | bytes 110596
  60.7 0.9 %copy-start.5 = (s32[2,512]{1,0:T(2,128)S(1)}, s32[2,512]{1,0:T(2,128)}, u32[]{:S(2)}) copy-start(s32[2,512]{1,0:T(2,128)} %send.1) | copy-start | bytes 12292
  61.6 6.1 %copy-start.2 = (bf16[592,768]{1,0:T(8,128)(2,1)S(1)}, bf16[592,768]{1,0:T(8,128)(2,1)}, u32[]{:S(2)}) copy-start(bf16[592,768]{1,0:T(8,128)(2,1)} %get-tuple-element.43.w) | copy-start | bytes 2727940
  61.6 6.1 %copy-start.6 = (f32[128,8,128]{2,1,0:T(8,128)S(1)}, f32[128,8,128]{2,1,0:T(8,128)}, u32[]{:S(2)}) copy-start(f32[128,8,128]{2,1,0:T(8,128)} %get-tuple-element.33.extra) | copy-start | bytes 1572868
  64.4 10.6 %collective-permute-start = (f32[4,128]{1,0:T(4,128)S(1)}, f32[4,128]{1,0:T(4,128)S(1)}, u32[]{:S(2)}, u32[]{:S(2)}) collective-permute-start(f32[4,128]{1,0:T(4,128)S(1)} %get-tuple-element.36), channel_id=1, source_target_pairs={{0,1},{1,0},{2,3},{3,2},{4,5},{5,4},{6,7},{7,6},{8,9},{9,8},{10,11... | collective-permute-start | bytes 6152 | tf_op jit(solution)/shard_map/ppermute | solution.py:35
  65.8 9.2 %collective-permute-start.1 = (f32[4,128]{1,0:T(4,128)S(1)}, f32[4,128]{1,0:T(4,128)S(1)}, u32[]{:S(2)}, u32[]{:S(2)}) collective-permute-start(f32[4,128]{1,0:T(4,128)S(1)} %get-tuple-element.37), channel_id=1, source_target_pairs={{1,2},{2,1},{3,4},{4,3},{5,6},{6,5},{7,8},{8,7},{9,10},{10,9},{11,... | collective-permute-start | bytes 6152 | tf_op jit(solution)/shard_map/ppermute | solution.py:35
  67.7 7.3 %copy-start = (bf16[384,1024]{1,0:T(8,128)(2,1)S(1)}, bf16[384,1024]{1,0:T(8,128)(2,1)}, u32[]{:S(2)}) copy-start(bf16[384,1024]{1,0:T(8,128)(2,1)} %get-tuple-element.38.rows_of) | copy-start | bytes 2359300
  67.7 7.3 %copy-start.1 = (f32[128,1024]{1,0:T(8,128)S(1)}, f32[128,1024]{1,0:T(8,128)}, u32[]{:S(2)}) copy-start(f32[128,1024]{1,0:T(8,128)} %get-tuple-element.39.lanes_of) | copy-start | bytes 1572868

commit v3 on v2

--- a/solution.py
+++ b/solution.py
@@ -24,7 +24,6 @@
 POOL_STRIDE = POOL_MAX + 8
 NEAR_W = (len(LIVE) + 3) * HEAD + COEFS
 BODY_OFF = sum(n - HEAD for n in PADDED[1:])
-BODY_ROWS = BODY_OFF + BODY
 NT = (((1,), (1,)), ((), ()))
 MIB = 1 << 20
 
@@ -89,7 +88,7 @@
     near = [
         jnp.where(lanes < min(n, NEAR), off[k, 0:HEAD, 0:128], 0.0) for k, n in enumerate(LIVE)
     ]
-    near += [pltpu.roll(divisor, 128 - COEFS - (DOFS - 128), 1)[:HEAD]]
+    near += [pltpu.roll(divisor, COEFS, 1)[:HEAD]]
     near += [units(HEAD, 0), units(HEAD, NEAR), units(COEFS, 128 - COEFS)]
     pool = [
         jnp.where(lanes < LIVE[k] - NEAR, off[k, 0:HEAD, NEAR:DOFS], 0.0) for k in (4, 3)
@@ -98,8 +97,9 @@
     body = [
         jnp.concatenate([off[k], pad], axis=1)[HEAD:n] for k, n in enumerate(PADDED) if k > 0
     ]
-    body += [jnp.concatenate([jnp.zeros((DOFS, 128), F32), divisor], axis=1)[HEAD:]]
-    return (jnp.concatenate(v, axis=0) for v in (near, pool, body))
+    at = 128 - 2 * COEFS
+    sums = divisor[HEAD:, at : at + COEFS]
+    return (jnp.concatenate(v, axis=0) for v in (near, pool, body, [sums]))
 
 
 def three_passes(w):
@@ -119,9 +119,9 @@
 
 def pack_kernel(
     owner_in, orders_in, at_in, flip_in, material_in, diag_in, mass_in, field_in, source_in, off_in,
-    out, extra, near_out, far_out, body_out, rows_out, lanes_out,
+    out, extra, near_out, far_out, body_out, sums_out, rows_out, lanes_out,
     owner, orders, at, flip, material, diag, mass, field, source, off,
-    near_w, far_w, body_w, rows_of, lanes_of,
+    near_w, far_w, body_w, sums_w, rows_of, lanes_of,
     t0, t1, t2, t3, whole, halves, merged, pool, table,
     slot_index, pool_index, slot_at, pool_at, in_sems, out_sems, index_sems,
 ):
@@ -150,6 +150,7 @@
         sends[-1].start()
 
     table[...] = jnp.zeros(table.shape, F32)
+    pool[...] = jnp.zeros(pool.shape, F32)
     for c in loads[0:2]:
         c.wait()
     own_row, order = owner[...], orders[...]
@@ -177,7 +178,7 @@
     rows_of[...] = mine.astype(F32).astype(BF16)
     spot = lax.broadcasted_iota(jnp.int32, (128, faces), 0) == lax.rem(row, 128)
     lanes_of[...] = jnp.where(spot, signs, 0.0)
-    first = DOFS + 4 - 128
+    first = 128 - 2 * COEFS + 4
     orders_held = len(LIVE)
     table[first : first + orders_held, 0:DOFS] = diag[...]
     table[first + orders_held : first + 2 * orders_held, 0:DOFS] = mass[...]
@@ -195,16 +196,18 @@
         top = jnp.where(order[:, here] == 4, field[NEAR + 64 : DOFS, here], source[NEAR : NEAR + 64, here])
         t2[here, :] = jnp.concatenate([field[NEAR : NEAR + 64, here], top], axis=0).T
         t3[here, :] = source[NEAR:DOFS, here].T
-    near, far, body = weights_of(off, table[...].T[:DOFS])
+    near, far, body, divisor = weights_of(off, table[...].T[:DOFS])
     near_w[...] = three_passes(near)
     far_w[...] = three_passes(far)
     body_w[...] = three_passes(body)
+    sums_w[...] = three_passes(divisor)
     for c in copies:
         c.wait()
     for src, dst in (
         (near_w, near_out),
         (far_w, far_out),
         (body_w, body_out),
+        (sums_w, sums_out),
         (rows_of, rows_out),
         (lanes_of, lanes_out),
     ):
@@ -243,7 +246,8 @@
     made = [
         jax.ShapeDtypeStruct((NEAR_W, 384), BF16),
         jax.ShapeDtypeStruct((2 * HEAD, 384), BF16),
-        jax.ShapeDtypeStruct((BODY_ROWS, 768), BF16),
+        jax.ShapeDtypeStruct((BODY_OFF, 768), BF16),
+        jax.ShapeDtypeStruct((BODY, 3 * COEFS), BF16),
         jax.ShapeDtypeStruct((HEAD * 16, faces), BF16),
         jax.ShapeDtypeStruct((128, faces), F32),
     ]
@@ -255,7 +259,7 @@
         ]
         + made,
         in_specs=[hbm] * len(operands),
-        out_specs=[hbm] * 7,
+        out_specs=[hbm] * 8,
         scratch_shapes=[pltpu.VMEM(a.shape, a.dtype) for a in list(operands) + made]
         + [pltpu.VMEM((count, 128), F32)] * 4
         + [pltpu.VMEM((owners * CAP, 128), F32)] * 2
@@ -268,7 +272,7 @@
             pltpu.SMEM((1, count), jnp.int32),
             pltpu.SMEM((1, count), jnp.int32),
             pltpu.SemaphoreType.DMA((len(operands),)),
-            pltpu.SemaphoreType.DMA((9,)),
+            pltpu.SemaphoreType.DMA((10,)),
             pltpu.SemaphoreType.DMA((2,)),
         ],
         compiler_params=pltpu.CompilerParams(vmem_limit_bytes=60 * MIB),
@@ -302,10 +306,8 @@
     return jnp.concatenate(tiles, axis=1)
 
 
-def field_pieces(values):
-    wide = values.shape[1]
-    full = jnp.concatenate([values, jnp.zeros((256 - values.shape[0], wide), F32)], axis=0)
-    hi, lo = two_pieces(full)
+def stacked_pieces(values):
+    hi, lo = two_pieces(values)
     return jnp.concatenate([hi, hi, lo], axis=0)
 
 
@@ -418,32 +420,43 @@
     )(recv, flag, extra, near_w, far_w, face_send)
 
 
-def body_kernel(recv, flag, extra, w, fresh, residual, more, sem):
-    t = pl.program_id(0)
-
-    @pl.when(t == 0)
-    def _():
-        load_overflow(flag, extra, more, sem)
-
-    group = recv.shape[0]
-    slots = group * CAP
-    near = recv[:, 0:CAP, :].reshape(-1, 128).T
-    middle = recv[:, CAP:NEAR_ROWS, :]
+def chosen_columns(pools, first_row):
+    held = pools.shape[1] * CAP // first_row.shape[1]
+    lane = lax.broadcasted_iota(jnp.int32, (1, 128), 1)
+    row = lax.broadcasted_iota(jnp.int32, (8 * held, 256), 0)
+    fars = []
+    for j in range(first_row.shape[1] // 128):
+        at = lane // CAP * held + first_row[:, j * 128 : (j + 1) * 128]
+        chosen = (row == jnp.concatenate([at, at + 1], axis=1)).astype(F32).astype(BF16)
+        hi, lo = two_pieces(pools[:, j * 8 * held : (j + 1) * 8 * held])
+        both = dot(jnp.concatenate([hi, lo], axis=0), chosen)
+        fars.append(both[0:128] + both[128:256])
+    return (
+        jnp.concatenate([f[:, i * 128 : (i + 1) * 128] for f in fars], axis=1) for i in range(2)
+    )
+
+
+def unpacked(recv, more, at):
+    near = recv[at, 0:CAP, :].reshape(-1, 128).T
+    middle = recv[at, CAP:NEAR_ROWS, :]
     turned = pltpu.roll(middle.reshape(-1, 128), 64, 1).reshape(middle.shape)
     middle = jnp.stack([middle, turned], axis=1).reshape(-1, 128).T[0:64]
-    rest = more[pl.ds(t * group, group), :, :]
-    pools = jnp.concatenate([recv[:, NEAR_ROWS:, :], rest], axis=1).reshape(-1, 128).T
+    pools = jnp.concatenate([recv[at, NEAR_ROWS:, :], more[at]], axis=1).reshape(-1, 128).T
     coefs = near[128 - COEFS :]
-    c0, live = coefs[0:1], coefs[2:3]
-    first_row = coefs[3:4].astype(jnp.int32)
-    far = pool_columns(pools, first_row)
-    far_rhs = pool_columns(pools, first_row + 1)
+    far, far_rhs = chosen_columns(pools, coefs[3:4].astype(jnp.int32))
+    slots = near.shape[1]
     rows = lax.broadcasted_iota(jnp.int32, (DOFS, slots), 0).astype(F32)
-    alive = rows + 0.5 < live
+    alive = rows + 0.5 < coefs[2:3]
     values = jnp.where(alive, jnp.concatenate([near[0:NEAR], far], axis=0), 0.0)
-    y = dot(w[...], field_pieces(jnp.concatenate([values, coefs], axis=0)))
     top = jnp.where(coefs[8:9] > 0.0, far_rhs[0:64], far[64:128])
     rhs = jnp.concatenate([middle, top, far_rhs[64:]], axis=0)
+    full = jnp.concatenate([values, jnp.zeros((256 - DOFS, slots), F32)], axis=0)
+    return stacked_pieces(full), stacked_pieces(coefs), coefs, values[HEAD:], rhs
+
+
+def body_step(off_w, sums_w, x, c, coefs, field, rhs):
+    y = dot(off_w[...], x)
+    c0, live = coefs[0:1], coefs[2:3]
     product = None
     start = BODY_OFF
     for k in range(len(LIVE) - 1, 0, -1):
@@ -455,35 +468,58 @@
         else:
             best = jnp.where(coefs[4 + k : 5 + k] > 0.0, mine, product[0:size])
             product = jnp.concatenate([best, product[size:]], axis=0)
-    alive = alive[HEAD:]
-    field = values[HEAD:]
-    divisor = jnp.where(alive, y[BODY_OFF:], 1.0)
+    rows = lax.broadcasted_iota(jnp.int32, field.shape, 0).astype(F32) + HEAD
+    alive = rows + 0.5 < live
+    divisor = jnp.where(alive, dot(sums_w[...], c), 1.0)
     left = jnp.where(alive, rhs - c0 * product - divisor * field, 0.0)
-    residual[HEAD:, :] = left
-    fresh[HEAD:, :] = field + CHEBY * left / divisor
-
-
-def body_rows(recv, flag, extra, w, group):
-    partners, rows = recv.shape[:2]
+    return field + CHEBY * left / divisor, left
+
+
+def body_kernel(recv, flag, extra, off_w, sums_w, fresh, residual, more, new, rest, sem, sems, *, group):
+    more[...] = jnp.zeros(more.shape, F32)
+    load_overflow(flag, extra, more, sem)
+    slots = group * CAP
+    steps = recv.shape[0] // group
+    sends = []
+    ready = unpacked(recv, more, slice(0, group))
+    for t in range(steps):
+        now = ready
+        if t + 1 < steps:
+            ready = unpacked(recv, more, slice((t + 1) * group, (t + 2) * group))
+        here = slice(t * slots, (t + 1) * slots)
+        new[:, here], rest[:, here] = body_step(off_w, sums_w, *now)
+        for src, dst in ((new, fresh), (rest, residual)):
+            sends.append(
+                pltpu.make_async_copy(
+                    src.at[:, here], dst.at[HEAD:DOFS, here], sems.at[len(sends)]
+                )
+            )
+            sends[-1].start()
+    for c in sends:
+        c.wait()
+
+
+def body_rows(recv, flag, extra, off_w, sums_w, group):
+    partners = recv.shape[0]
     slots = partners * CAP
     vmem = pl.BlockSpec(memory_space=pltpu.VMEM)
-    wide = pl.BlockSpec((DOFS, group * CAP), lambda t: (0, t))
+    hbm = pl.BlockSpec(memory_space=pltpu.HBM)
     return pl.pallas_call(
-        body_kernel,
-        grid=(partners // group,),
+        functools.partial(body_kernel, group=group),
         out_shape=[jax.ShapeDtypeStruct((DOFS, slots), F32)] * 2,
-        in_specs=[
-            pl.BlockSpec((group, rows, 128), lambda t: (t, 0, 0)),
-            vmem,
-            pl.BlockSpec(memory_space=pltpu.HBM),
-            vmem,
+        in_specs=[vmem, vmem, hbm, vmem, vmem],
+        out_specs=[hbm] * 2,
+        scratch_shapes=[
+            pltpu.VMEM(extra.shape, F32),
+            pltpu.VMEM((BODY, slots), F32),
+            pltpu.VMEM((BODY, slots), F32),
+            pltpu.SemaphoreType.DMA,
+            pltpu.SemaphoreType.DMA((2 * partners // group,)),
         ],
-        out_specs=[wide] * 2,
-        scratch_shapes=[pltpu.VMEM(extra.shape, F32), pltpu.SemaphoreType.DMA],
         compiler_params=pltpu.CompilerParams(vmem_limit_bytes=24 * MIB),
         cost_estimate=pl.CostEstimate(flops=4 * 10**9, bytes_accessed=8 * 10**6, transcendentals=0),
         name="body_rows",
-    )(recv, flag, extra, w)
+    )(recv, flag, extra, off_w, sums_w)
 
 
 def finish_kernel(one, two, rows_of, lanes_of, base, field, step, _, __, fresh, residual, flat):
@@ -537,7 +573,7 @@
 ):
     count = iterate.shape[1]
     owners = lax.axis_size("grp") * lax.axis_size("dev")
-    packed, extra, near_w, far_w, body_w, rows_of, lanes_of = pack(
+    packed, extra, near_w, far_w, off_w, sums_w, rows_of, lanes_of = pack(
         (
             new_owner.reshape(1, count),
             orders.reshape(1, count),
@@ -565,7 +601,7 @@
     )
     base, field, step, one, two = head_rows(recv, same, extra, near_w, far_w, face_send, 16)
     one, two = swapped(one, "dev", 0), swapped(two, "dev", 1)
-    fresh, residual = body_rows(recv, same, extra, body_w, 32)
+    fresh, residual = body_rows(recv, same, extra, off_w, sums_w, 32)
     return tuple(finish(one, two, rows_of, lanes_of, base, field, step, fresh, residual))
 
 

time: 76.7 us -> 74.4 us (0.970)
  Pallas kernels: 18.5 us -> 16.2 us
    pallas_call x1, Pallas kernels: 7.21 us -> 5.01 us  [body_rows(): pl.pallas_call(functools.partial(body_kernel, group=group), out_shape=[ja...]
  transfers between devices with their start and end apart: 2 -> 2, of which waited for: 0 -> 0; matrix products, arithmetic and copies ran while one was open for 0% -> 0% of each run, Pallas kernels for 9% -> 7%
where the time goes in v3:
time: 74.4 us; the launch traced here: 74.1 us
  blocking collectives  52.9 us (71%)
  Pallas kernels  16.2 us (22%)
  starting transfers between devices  3.3 us (4%)
  between operations  0.76 us (1%)
    all_to_all x1, blocking collectives, exchanged(): lax.all_to_all(rows, ('grp', 'dev'), split_axis=0, concat_axis=0, tiled=T...  52.9 us
    pallas_call x1, Pallas kernels, pack(): pl.pallas_call(pack_kernel, out_shape=[jax.ShapeDtypeStruct((owners, NEAR...  6.41 us
    pallas_call x1, Pallas kernels, body_rows(): pl.pallas_call(functools.partial(body_kernel, group=group), out_shape=[ja...  5.01 us
    ppermute x2, starting transfers between devices, swapped(): lax.ppermute(array, axis, [p for i in lower for p in ((i, i + 1), (i + 1,...  3.3 us
    pallas_call x1, Pallas kernels, head_rows(): pl.pallas_call(functools.partial(head_kernel, group=group), out_shape=[ja...  2.64 us
  transfers between devices with their start and end apart: 2, of which 0 were waited for; matrix products, arithmetic and copies ran while one was open for 0% of the time, Pallas kernels for 7%

profile of v3, /device:TPU:1, one launch (start us, length us, event | category | flops | bytes accessed | tf_op | source)
XLA Modules:
  0.0 74.1 jit_solution(6257765944662060633)
XLA Ops:
  0.6 6.4 %pack.1 = (f32[128,48,128]{2,1,0:T(8,128)}, f32[128,8,128]{2,1,0:T(8,128)}, bf16[208,384]{1,0:T(8,128)(2,1)}, bf16[48,384]{1,0:T(8,128)(2,1)}, bf16[400,768]{1,0...) custom-call(s32[1,1024]{1,0:T(1,128)} %bitcast.3, s32[1,1024]{1,0:T(1,128)} %bitcast.4, ...), custom_call_target="tpu_custom_call" | custom-call | tf_op jit(solution)/shard_map/pack/pallas_call | solution.py:254
  7.0 52.9 %all_to_all.9.recv = f32[128,48,128]{2,1,0:T(8,128)S(1)} all-to-all(f32[128,48,128]{2,1,0:T(8,128)} %get-tuple-element.30), channel_id=1, replica_groups=mesh['grp'=4,'dev'=32] {'grp','dev'}, dimensions={0} | all-to-all | bytes 6291456 | tf_op jit(solution)/shard_map/all_to_all | solution.py:593
  60.0 0.7 %flag_of.1 = (f32[1,1]{1,0:T(1,128)}, f32[1,1]{1,0:T(1,128)}) custom-call(f32[128,48,128]{2,1,0:T(8,128)S(1)} %all_to_all.9.recv), custom_call_target="tpu_custom_call" | custom-call | tf_op jit(solution)/shard_map/flag_of/pallas_call | solution.py:323
  60.7 0.0 copy-start.3
  60.7 0.0 copy-start.5
  60.7 0.7 while.9
  61.4 0.2 copy-done.3
  61.6 0.0 copy-done.5
  61.6 0.0 copy-done.6
  61.7 0.0 copy-start.7
  61.7 2.6 %head_rows.1 = (f32[24,2048]{1,0:T(8,128)S(1)}, f32[24,2048]{1,0:T(8,128)S(1)}, f32[24,2048]{1,0:T(8,128)S(1)}, f32[4,128]{1,0:T(4,128)S(1)}, f32[4,128]{1,0:T(4,128)S(1)}) custom-call(f32[128,48,128]{2,1,0:T(8,128)S(1)} %all_to_all.9.recv, f32[1,1]{1,0:T(1,128)} %get-tuple-element.31.flag, f32[128,8,128]{2,1,0:T(8,128)} %get-tuple-element.34.extra, ...), custom_call_target="tpu_custom_call" | custom-call | flops 2000000000 | bytes 4000000 | tf_op jit(solution)/shard_map/head_rows/pallas_call | solution.py:406
  64.3 1.4 %collective-permute-start = (f32[4,128]{1,0:T(4,128)S(1)}, f32[4,128]{1,0:T(4,128)S(1)}, u32[]{:S(2)}, u32[]{:S(2)}) collective-permute-start(f32[4,128]{1,0:T(4,128)S(1)} %get-tuple-element.37), channel_id=1, source_target_pairs={{0,1},{1,0},{2,3},{3,2},{4,5},{5,4},{6,7},{7,6},{8,9},{9,8},{10,11... | collective-permute-start | bytes 6152 | tf_op jit(solution)/shard_map/ppermute | solution.py:34
  65.7 1.9 %collective-permute-start.1 = (f32[4,128]{1,0:T(4,128)S(1)}, f32[4,128]{1,0:T(4,128)S(1)}, u32[]{:S(2)}, u32[]{:S(2)}) collective-permute-start(f32[4,128]{1,0:T(4,128)S(1)} %get-tuple-element.38), channel_id=1, source_target_pairs={{1,2},{2,1},{3,4},{4,3},{5,6},{6,5},{7,8},{8,7},{9,10},{10,9},{11,... | collective-permute-start | bytes 6152 | tf_op jit(solution)/shard_map/ppermute | solution.py:34
  67.6 0.0 copy-done.2
  67.6 0.0 copy-done.4
  67.7 0.0 copy-done.7
  67.7 0.0 copy-start
  67.7 0.0 copy-start.1
  67.7 5.0 %body_rows.1 = (f32[216,2048]{1,0:T(8,128)}, f32[216,2048]{1,0:T(8,128)}) custom-call(f32[128,48,128]{2,1,0:T(8,128)S(1)} %all_to_all.9.recv, f32[1,1]{1,0:T(1,128)} %get-tuple-element.31.flag, f32[128,8,128]{2,1,0:T(8,128)S(1)} %copy-done.7, bf16[400,768]{1,0:T(8,128)(2,1)S(1)} %copy-done.2, bf16[192,48]{1,0:T(8,128)(2,1)S(1)} %copy-done.4), custom_call_target="tpu_custom_call" | custom-call | flops 4000000000 | bytes 8000000 | tf_op jit(solution)/shard_map/body_rows/pallas_call | solution.py:507
  72.7 0.0 collective-permute-done.one
  72.7 0.0 collective-permute-done.1.two
  72.7 0.0 copy-done
  72.7 0.0 copy-done.1
  72.7 1.4 %finish.1 = (f32[216,2048]{1,0:T(8,128)}, f32[216,2048]{1,0:T(8,128)}) custom-call(f32[4,128]{1,0:T(4,128)S(1)} %collective-permute-done.one, f32[4,128]{1,0:T(4,128)S(1)} %collective-permute-done.1.two, bf16[384,1024]{1,0:T(8,128)(2,1)S(1)} %copy-done, f32[128,1024]{1,0:T(8,128)S(1)} %copy-done.1, ...), custom_call_target="tpu_custom_call", output_to_operand_aliasing={{0}: (7, {}), {1}: (8, {})} | custom-call | flops 1000000000 | bytes 1000000 | tf_op jit(solution)/shard_map/finish/pallas_call | solution.py:547
  (3 shorter events, 0.0 us)
Async XLA Ops:
  60.7 0.9 %copy-start.3 = (bf16[208,384]{1,0:T(8,128)(2,1)S(1)}, bf16[208,384]{1,0:T(8,128)(2,1)}, u32[]{:S(2)}) copy-start(bf16[208,384]{1,0:T(8,128)(2,1)} %get-tuple-element.35.near_w) | copy-start | bytes 479236
  60.7 0.9 %copy-start.5 = (bf16[48,384]{1,0:T(8,128)(2,1)S(1)}, bf16[48,384]{1,0:T(8,128)(2,1)}, u32[]{:S(2)}) copy-start(bf16[48,384]{1,0:T(8,128)(2,1)} %get-tuple-element.36.far_w) | copy-start | bytes 110596
  60.7 0.9 %copy-start.6 = (s32[2,512]{1,0:T(2,128)S(1)}, s32[2,512]{1,0:T(2,128)}, u32[]{:S(2)}) copy-start(s32[2,512]{1,0:T(2,128)} %send.1) | copy-start | bytes 12292
  61.7 6.0 %copy-start.2 = (bf16[400,768]{1,0:T(8,128)(2,1)S(1)}, bf16[400,768]{1,0:T(8,128)(2,1)}, u32[]{:S(2)}) copy-start(bf16[400,768]{1,0:T(8,128)(2,1)} %get-tuple-element.44.off_w) | copy-start | bytes 1843204
  61.7 6.0 %copy-start.4 = (bf16[192,48]{1,0:T(8,128)(2,1)S(1)}, bf16[192,48]{1,0:T(8,128)(2,1)}, u32[]{:S(2)}) copy-start(bf16[192,48]{1,0:T(8,128)(2,1)} %get-tuple-element.45.sums_w) | copy-start | bytes 55300
  61.7 6.0 %copy-start.7 = (f32[128,8,128]{2,1,0:T(8,128)S(1)}, f32[128,8,128]{2,1,0:T(8,128)}, u32[]{:S(2)}) copy-start(f32[128,8,128]{2,1,0:T(8,128)} %get-tuple-element.34.extra) | copy-start | bytes 1572868
  64.3 8.4 %collective-permute-start = (f32[4,128]{1,0:T(4,128)S(1)}, f32[4,128]{1,0:T(4,128)S(1)}, u32[]{:S(2)}, u32[]{:S(2)}) collective-permute-start(f32[4,128]{1,0:T(4,128)S(1)} %get-tuple-element.37), channel_id=1, source_target_pairs={{0,1},{1,0},{2,3},{3,2},{4,5},{5,4},{6,7},{7,6},{8,9},{9,8},{10,11... | collective-permute-start | bytes 6152 | tf_op jit(solution)/shard_map/ppermute | solution.py:34
  65.7 7.0 %collective-permute-start.1 = (f32[4,128]{1,0:T(4,128)S(1)}, f32[4,128]{1,0:T(4,128)S(1)}, u32[]{:S(2)}, u32[]{:S(2)}) collective-permute-start(f32[4,128]{1,0:T(4,128)S(1)} %get-tuple-element.38), channel_id=1, source_target_pairs={{1,2},{2,1},{3,4},{4,3},{5,6},{6,5},{7,8},{8,7},{9,10},{10,9},{11,... | collective-permute-start | bytes 6152 | tf_op jit(solution)/shard_map/ppermute | solution.py:34
  67.7 5.1 %copy-start = (bf16[384,1024]{1,0:T(8,128)(2,1)S(1)}, bf16[384,1024]{1,0:T(8,128)(2,1)}, u32[]{:S(2)}) copy-start(bf16[384,1024]{1,0:T(8,128)(2,1)} %get-tuple-element.39.rows_of) | copy-start | bytes 2359300
  67.7 5.1 %copy-start.1 = (f32[128,1024]{1,0:T(8,128)S(1)}, f32[128,1024]{1,0:T(8,128)}, u32[]{:S(2)}) copy-start(f32[128,1024]{1,0:T(8,128)} %get-tuple-element.40.lanes_of) | copy-start | bytes 1572868

commit v4 on v3

--- a/solution.py
+++ b/solution.py
@@ -93,10 +93,11 @@
     pool = [
         jnp.where(lanes < LIVE[k] - NEAR, off[k, 0:HEAD, NEAR:DOFS], 0.0) for k in (4, 3)
     ]
-    pad = jnp.zeros((DOFS, 256 - DOFS), F32)
-    body = [
-        jnp.concatenate([off[k], pad], axis=1)[HEAD:n] for k, n in enumerate(PADDED) if k > 0
-    ]
+    body = []
+    for k, n in enumerate(PADDED[1:], 1):
+        wide = 128 if n < 128 else DOFS
+        pad = jnp.zeros((n - HEAD, 256 - wide), F32)
+        body.append(jnp.concatenate([off[k, HEAD:n, 0:wide], pad], axis=1))
     at = 128 - 2 * COEFS
     sums = divisor[HEAD:, at : at + COEFS]
     return (jnp.concatenate(v, axis=0) for v in (near, pool, body, [sums]))
@@ -123,13 +124,13 @@
     owner, orders, at, flip, material, diag, mass, field, source, off,
     near_w, far_w, body_w, sums_w, rows_of, lanes_of,
     t0, t1, t2, t3, whole, halves, merged, pool, table,
-    slot_index, pool_index, slot_at, pool_at, in_sems, out_sems, index_sems,
+    coefs_at, slot_index, pool_index, slot_at, pool_at, in_sems, out_sems, index_sems, spill_sem,
 ):
     count = field.shape[1]
     owners = out.shape[0]
     chunk = 128
     loads = []
-    for src, dst in (
+    pairs = [
         (owner_in, owner),
         (orders_in, orders),
         (at_in, at),
@@ -139,8 +140,11 @@
         (mass_in, mass),
         (field_in, field),
         (source_in, source),
-        (off_in, off),
-    ):
+    ]
+    for k, n in enumerate(PADDED):
+        part = slice(0, n), slice(0, 128 if n < 128 else DOFS)
+        pairs.append((off_in.at[k, part[0], part[1]], off.at[k, part[0], part[1]]))
+    for src, dst in pairs:
         loads.append(pltpu.make_async_copy(src, dst, in_sems.at[len(loads)]))
         loads[-1].start()
     sends = []
@@ -177,22 +181,17 @@
     mine = lax.broadcasted_iota(jnp.int32, (HEAD * 16, faces), 0) == row // 128
     rows_of[...] = mine.astype(F32).astype(BF16)
     spot = lax.broadcasted_iota(jnp.int32, (128, faces), 0) == lax.rem(row, 128)
-    lanes_of[...] = jnp.where(spot, signs, 0.0)
+    lanes_of[...] = jnp.where(spot, signs, 0.0).astype(BF16)
     first = 128 - 2 * COEFS + 4
     orders_held = len(LIVE)
     table[first : first + orders_held, 0:DOFS] = diag[...]
     table[first + orders_held : first + 2 * orders_held, 0:DOFS] = mass[...]
-    coefs = coefficients(material[...], order, first_row, overflow)
+    coefs_at[...] = coefficients(material[...], order, first_row, overflow)
 
     for c in loads[7:]:
         c.wait()
     for c in range(count // chunk):
         here = slice(c * chunk, (c + 1) * chunk)
-        t0[here, :] = jnp.concatenate(
-            [field[0:NEAR, here], source[0:HEAD, here], coefs[:, here]], axis=0
-        ).T
-        middle = source[HEAD:NEAR, here]
-        t1[here, :] = jnp.concatenate([middle, middle], axis=0).T
         top = jnp.where(order[:, here] == 4, field[NEAR + 64 : DOFS, here], source[NEAR : NEAR + 64, here])
         t2[here, :] = jnp.concatenate([field[NEAR : NEAR + 64, here], top], axis=0).T
         t3[here, :] = source[NEAR:DOFS, here].T
@@ -213,22 +212,36 @@
     ):
         send(src, dst)
 
-    def place(row_at, steps):
+    def place(row_at, steps, size, also=None):
         def step(g, carry):
-            for j in range(32):
-                i = g * 32 + j
+            if also is not None:
+                also(pl.ds(pl.multiple_of(g * size, size), size))
+            for j in range(size):
+                i = g * size + j
                 row = row_at[0, i]
                 for rows, block, ahead in steps:
                     block[pl.ds(row + ahead, 1), :] = rows[pl.ds(i, 1), :]
             return carry
 
-        lax.fori_loop(0, count // 32, step, 0)
-
-    place(pool_at, [(t2, pool, 0), (t3, pool, 1)])
+        lax.fori_loop(0, count // size, step, 0)
+
+    def turn(here):
+        t0[here, :] = jnp.concatenate(
+            [field[0:NEAR, here], source[0:HEAD, here], coefs_at[:, here]], axis=0
+        ).T
+        middle = source[HEAD:NEAR, here]
+        t1[here, :] = jnp.concatenate([middle, middle], axis=0).T
+
+    place(pool_at, [(t2, pool, 0), (t3, pool, 1)], chunk, turn)
     pools = pool.reshape(owners, POOL_STRIDE, 128)
     send(pools.at[:, 0:POOL, :], out.at[:, NEAR_ROWS : NEAR_ROWS + POOL, :])
-    send(pools.at[:, POOL:POOL_MAX, :], extra)
-    place(slot_at, [(t0, whole, 0), (t1, halves, 0)])
+    spill = pltpu.make_async_copy(pools.at[:, POOL:POOL_MAX, :], extra, spill_sem)
+
+    @pl.when(overflow > 0.5)
+    def _():
+        spill.start()
+
+    place(slot_at, [(t0, whole, 0), (t1, halves, 0)], 64)
     send(whole.reshape(owners, CAP, 128), out.at[:, 0:CAP, :])
     both = halves[...].reshape(owners, CAP, 128)
     low = lax.broadcasted_iota(jnp.int32, (owners, CAP // 2, 128), 2) < 64
@@ -237,6 +250,10 @@
     send(merged.reshape(owners, CAP // 2, 128), out.at[:, CAP:NEAR_ROWS, :])
     for c in sends:
         c.wait()
+
+    @pl.when(overflow > 0.5)
+    def _():
+        spill.wait()
 
 
 def pack(operands, owners):
@@ -249,7 +266,7 @@
         jax.ShapeDtypeStruct((BODY_OFF, 768), BF16),
         jax.ShapeDtypeStruct((BODY, 3 * COEFS), BF16),
         jax.ShapeDtypeStruct((HEAD * 16, faces), BF16),
-        jax.ShapeDtypeStruct((128, faces), F32),
+        jax.ShapeDtypeStruct((128, faces), BF16),
     ]
     return pl.pallas_call(
         pack_kernel,
@@ -267,13 +284,15 @@
             pltpu.VMEM((owners * CAP // 2, 128), F32),
             pltpu.VMEM((owners * POOL_STRIDE, 128), F32),
             pltpu.VMEM((128, 256), F32),
+            pltpu.VMEM((COEFS, count), F32),
             pltpu.VMEM((1, count), jnp.int32),
             pltpu.VMEM((1, count), jnp.int32),
             pltpu.SMEM((1, count), jnp.int32),
             pltpu.SMEM((1, count), jnp.int32),
-            pltpu.SemaphoreType.DMA((len(operands),)),
-            pltpu.SemaphoreType.DMA((10,)),
+            pltpu.SemaphoreType.DMA((len(operands) - 1 + len(LIVE),)),
+            pltpu.SemaphoreType.DMA((9,)),
             pltpu.SemaphoreType.DMA((2,)),
+            pltpu.SemaphoreType.DMA,
         ],
         compiler_params=pltpu.CompilerParams(vmem_limit_bytes=60 * MIB),
         name="pack",
@@ -526,10 +545,11 @@
     values = jnp.concatenate(
         [one[i : i + 1, :] for i in range(4)] + [two[i : i + 1, :] for i in range(4)], axis=1
     )
-    hi, mid = (p.astype(F32) for p in two_pieces(values))
+    hi, mid = two_pieces(values)
+    low = (values - hi.astype(F32) - mid.astype(F32)).astype(BF16)
     spread = lanes_of[...]
-    pieces = jnp.concatenate([spread * hi, spread * mid, spread * (values - hi - mid)], axis=0)
-    found = dot(rows_of[...], pieces.astype(BF16), NT)
+    pieces = jnp.concatenate([spread * hi, spread * mid, spread * low], axis=0)
+    found = dot(rows_of[...], pieces, NT)
     flat[...] = found[:, 0:128] + found[:, 128:256] + found[:, 256:384]
     for b in range(16):
         at = slice(b * 128, (b + 1) * 128)

time: 74.4 us -> 73.8 us (level)
  no operation moved by 1% of the time
where the time goes in v4:
time: 73.8 us; the launch traced here: 73.5 us
  blocking collectives  52.9 us (72%)
  Pallas kernels  15.6 us (21%)
  starting transfers between devices  3.3 us (4%)
  between operations  0.76 us (1%)
    all_to_all x1, blocking collectives, exchanged(): lax.all_to_all(rows, ('grp', 'dev'), split_axis=0, concat_axis=0, tiled=T...  52.9 us
    pallas_call x1, Pallas kernels, pack(): pl.pallas_call(pack_kernel, out_shape=[jax.ShapeDtypeStruct((owners, NEAR...  5.84 us
    pallas_call x1, Pallas kernels, body_rows(): pl.pallas_call(functools.partial(body_kernel, group=group), out_shape=[ja...  4.99 us
    ppermute x2, starting transfers between devices, swapped(): lax.ppermute(array, axis, [p for i in lower for p in ((i, i + 1), (i + 1,...  3.3 us
    pallas_call x1, Pallas kernels, head_rows(): pl.pallas_call(functools.partial(head_kernel, group=group), out_shape=[ja...  2.64 us
  transfers between devices with their start and end apart: 2, of which 0 were waited for; matrix products, arithmetic and copies ran while one was open for 0% of the time, Pallas kernels for 7%

profile of v4, /device:TPU:1, one launch (start us, length us, event | category | flops | bytes accessed | tf_op | source)
XLA Modules:
  0.0 73.5 jit_solution(16011405919095569845)
XLA Ops:
  0.6 5.8 %pack.1 = (f32[128,48,128]{2,1,0:T(8,128)}, f32[128,8,128]{2,1,0:T(8,128)}, bf16[208,384]{1,0:T(8,128)(2,1)}, bf16[48,384]{1,0:T(8,128)(2,1)}, bf16[400,768]{1,0...) custom-call(s32[1,1024]{1,0:T(1,128)} %bitcast.3, ...), custom_call_target="tpu_custom_call" | custom-call | tf_op jit(solution)/shard_map/pack/pallas_call | solution.py:271
  6.5 52.9 %all_to_all.9.recv = f32[128,48,128]{2,1,0:T(8,128)S(1)} all-to-all(f32[128,48,128]{2,1,0:T(8,128)} %get-tuple-element.30), channel_id=1, replica_groups=mesh['grp'=4,'dev'=32] {'grp','dev'}, dimensions={0} | all-to-all | bytes 6291456 | tf_op jit(solution)/shard_map/all_to_all | solution.py:613
  59.4 0.7 %flag_of.1 = (f32[1,1]{1,0:T(1,128)}, f32[1,1]{1,0:T(1,128)}) custom-call(f32[128,48,128]{2,1,0:T(8,128)S(1)} %all_to_all.9.recv), custom_call_target="tpu_custom_call" | custom-call | tf_op jit(solution)/shard_map/flag_of/pallas_call | solution.py:342
  60.2 0.0 copy-start.3
  60.2 0.0 copy-start.5
  60.2 0.7 while.9
  60.9 0.2 copy-done.3
  61.1 0.0 copy-done.5
  61.1 0.0 copy-done.6
  61.1 0.0 copy-start.7
  61.1 2.6 %head_rows.1 = (f32[24,2048]{1,0:T(8,128)S(1)}, f32[24,2048]{1,0:T(8,128)S(1)}, f32[24,2048]{1,0:T(8,128)S(1)}, f32[4,128]{1,0:T(4,128)S(1)}, f32[4,128]{1,0:T(4,128)S(1)}) custom-call(f32[128,48,128]{2,1,0:T(8,128)S(1)} %all_to_all.9.recv, f32[1,1]{1,0:T(1,128)} %get-tuple-element.31.flag, f32[128,8,128]{2,1,0:T(8,128)} %get-tuple-element.34.extra, ...), custom_call_target="tpu_custom_call" | custom-call | flops 2000000000 | bytes 4000000 | tf_op jit(solution)/shard_map/head_rows/pallas_call | solution.py:425
  63.7 1.4 %collective-permute-start = (f32[4,128]{1,0:T(4,128)S(1)}, f32[4,128]{1,0:T(4,128)S(1)}, u32[]{:S(2)}, u32[]{:S(2)}) collective-permute-start(f32[4,128]{1,0:T(4,128)S(1)} %get-tuple-element.37), channel_id=1, source_target_pairs={{0,1},{1,0},{2,3},{3,2},{4,5},{5,4},{6,7},{7,6},{8,9},{9,8},{10,11... | collective-permute-start | bytes 6152 | tf_op jit(solution)/shard_map/ppermute | solution.py:34
  65.1 1.9 %collective-permute-start.1 = (f32[4,128]{1,0:T(4,128)S(1)}, f32[4,128]{1,0:T(4,128)S(1)}, u32[]{:S(2)}, u32[]{:S(2)}) collective-permute-start(f32[4,128]{1,0:T(4,128)S(1)} %get-tuple-element.38), channel_id=1, source_target_pairs={{1,2},{2,1},{3,4},{4,3},{5,6},{6,5},{7,8},{8,7},{9,10},{10,9},{11,... | collective-permute-start | bytes 6152 | tf_op jit(solution)/shard_map/ppermute | solution.py:34
  67.1 0.0 copy-done.2
  67.1 0.0 copy-done.4
  67.1 0.0 copy-done.7
  67.1 0.0 copy-start
  67.1 0.0 copy-start.1
  67.1 5.0 %body_rows.1 = (f32[216,2048]{1,0:T(8,128)}, f32[216,2048]{1,0:T(8,128)}) custom-call(f32[128,48,128]{2,1,0:T(8,128)S(1)} %all_to_all.9.recv, f32[1,1]{1,0:T(1,128)} %get-tuple-element.31.flag, f32[128,8,128]{2,1,0:T(8,128)S(1)} %copy-done.7, bf16[400,768]{1,0:T(8,128)(2,1)S(1)} %copy-done.2, bf16[192,48]{1,0:T(8,128)(2,1)S(1)} %copy-done.4), custom_call_target="tpu_custom_call" | custom-call | flops 4000000000 | bytes 8000000 | tf_op jit(solution)/shard_map/body_rows/pallas_call | solution.py:526
  72.1 0.0 collective-permute-done.one
  72.1 0.0 collective-permute-done.1.two
  72.1 0.0 copy-done
  72.1 0.0 copy-done.1
  72.2 1.4 %finish.1 = (f32[216,2048]{1,0:T(8,128)}, f32[216,2048]{1,0:T(8,128)}) custom-call(f32[4,128]{1,0:T(4,128)S(1)} %collective-permute-done.one, f32[4,128]{1,0:T(4,128)S(1)} %collective-permute-done.1.two, bf16[384,1024]{1,0:T(8,128)(2,1)S(1)} %copy-done, bf16[128,1024]{1,0:T(8,128)(2,1)S(1)} %copy-done.1, ...), custom_call_target="tpu_custom_call", output_to_operand_aliasing={{0}: (7, {}), {1}: (8, {})} | custom-call | flops 1000000000 | bytes 1000000 | tf_op jit(solution)/shard_map/finish/pallas_call | solution.py:567
  (3 shorter events, 0.0 us)
Async XLA Ops:
  60.2 0.9 %copy-start.3 = (bf16[208,384]{1,0:T(8,128)(2,1)S(1)}, bf16[208,384]{1,0:T(8,128)(2,1)}, u32[]{:S(2)}) copy-start(bf16[208,384]{1,0:T(8,128)(2,1)} %get-tuple-element.35.near_w) | copy-start | bytes 479236
  60.2 0.9 %copy-start.5 = (bf16[48,384]{1,0:T(8,128)(2,1)S(1)}, bf16[48,384]{1,0:T(8,128)(2,1)}, u32[]{:S(2)}) copy-start(bf16[48,384]{1,0:T(8,128)(2,1)} %get-tuple-element.36.far_w) | copy-start | bytes 110596
  60.2 0.9 %copy-start.6 = (s32[2,512]{1,0:T(2,128)S(1)}, s32[2,512]{1,0:T(2,128)}, u32[]{:S(2)}) copy-start(s32[2,512]{1,0:T(2,128)} %send.1) | copy-start | bytes 12292
  61.1 6.0 %copy-start.2 = (bf16[400,768]{1,0:T(8,128)(2,1)S(1)}, bf16[400,768]{1,0:T(8,128)(2,1)}, u32[]{:S(2)}) copy-start(bf16[400,768]{1,0:T(8,128)(2,1)} %get-tuple-element.44.off_w) | copy-start | bytes 1843204
  61.1 6.0 %copy-start.4 = (bf16[192,48]{1,0:T(8,128)(2,1)S(1)}, bf16[192,48]{1,0:T(8,128)(2,1)}, u32[]{:S(2)}) copy-start(bf16[192,48]{1,0:T(8,128)(2,1)} %get-tuple-element.45.sums_w) | copy-start | bytes 55300
  61.1 6.0 %copy-start.7 = (f32[128,8,128]{2,1,0:T(8,128)S(1)}, f32[128,8,128]{2,1,0:T(8,128)}, u32[]{:S(2)}) copy-start(f32[128,8,128]{2,1,0:T(8,128)} %get-tuple-element.34.extra) | copy-start | bytes 1572868
  63.7 8.4 %collective-permute-start = (f32[4,128]{1,0:T(4,128)S(1)}, f32[4,128]{1,0:T(4,128)S(1)}, u32[]{:S(2)}, u32[]{:S(2)}) collective-permute-start(f32[4,128]{1,0:T(4,128)S(1)} %get-tuple-element.37), channel_id=1, source_target_pairs={{0,1},{1,0},{2,3},{3,2},{4,5},{5,4},{6,7},{7,6},{8,9},{9,8},{10,11... | collective-permute-start | bytes 6152 | tf_op jit(solution)/shard_map/ppermute | solution.py:34
  65.1 7.0 %collective-permute-start.1 = (f32[4,128]{1,0:T(4,128)S(1)}, f32[4,128]{1,0:T(4,128)S(1)}, u32[]{:S(2)}, u32[]{:S(2)}) collective-permute-start(f32[4,128]{1,0:T(4,128)S(1)} %get-tuple-element.38), channel_id=1, source_target_pairs={{1,2},{2,1},{3,4},{4,3},{5,6},{6,5},{7,8},{8,7},{9,10},{10,9},{11,... | collective-permute-start | bytes 6152 | tf_op jit(solution)/shard_map/ppermute | solution.py:34
  67.1 5.0 %copy-start = (bf16[384,1024]{1,0:T(8,128)(2,1)S(1)}, bf16[384,1024]{1,0:T(8,128)(2,1)}, u32[]{:S(2)}) copy-start(bf16[384,1024]{1,0:T(8,128)(2,1)} %get-tuple-element.39.rows_of) | copy-start | bytes 2359300
  67.1 5.0 %copy-start.1 = (bf16[128,1024]{1,0:T(8,128)(2,1)S(1)}, bf16[128,1024]{1,0:T(8,128)(2,1)}, u32[]{:S(2)}) copy-start(bf16[128,1024]{1,0:T(8,128)(2,1)} %get-tuple-element.40.lanes_of) | copy-start | bytes 786436

commit v5 on v4

--- a/solution.py
+++ b/solution.py
@@ -26,6 +26,7 @@
 BODY_OFF = sum(n - HEAD for n in PADDED[1:])
 NT = (((1,), (1,)), ((), ()))
 MIB = 1 << 20
+EARLY = 96
 
 
 def swapped(array, axis, first):
@@ -494,54 +495,54 @@
     return field + CHEBY * left / divisor, left
 
 
-def body_kernel(recv, flag, extra, off_w, sums_w, fresh, residual, more, new, rest, sem, sems, *, group):
-    more[...] = jnp.zeros(more.shape, F32)
-    load_overflow(flag, extra, more, sem)
+def body_blocks(recv, more, off_w, sums_w, fresh, residual, new, rest, sems, start, stop, group):
     slots = group * CAP
-    steps = recv.shape[0] // group
     sends = []
-    ready = unpacked(recv, more, slice(0, group))
-    for t in range(steps):
+    ready = unpacked(recv, more, slice(start, start + group))
+    for p in range(start, stop, group):
         now = ready
-        if t + 1 < steps:
-            ready = unpacked(recv, more, slice((t + 1) * group, (t + 2) * group))
-        here = slice(t * slots, (t + 1) * slots)
+        if p + group < stop:
+            ready = unpacked(recv, more, slice(p + group, p + 2 * group))
+        here = slice((p - start) * CAP, (p - start) * CAP + slots)
+        there = slice(p * CAP, p * CAP + slots)
         new[:, here], rest[:, here] = body_step(off_w, sums_w, *now)
         for src, dst in ((new, fresh), (rest, residual)):
             sends.append(
                 pltpu.make_async_copy(
-                    src.at[:, here], dst.at[HEAD:DOFS, here], sems.at[len(sends)]
+                    src.at[:, here], dst.at[HEAD:DOFS, there], sems.at[len(sends)]
                 )
             )
             sends[-1].start()
-    for c in sends:
-        c.wait()
-
-
-def body_rows(recv, flag, extra, off_w, sums_w, group):
-    partners = recv.shape[0]
-    slots = partners * CAP
-    vmem = pl.BlockSpec(memory_space=pltpu.VMEM)
-    hbm = pl.BlockSpec(memory_space=pltpu.HBM)
-    return pl.pallas_call(
-        functools.partial(body_kernel, group=group),
-        out_shape=[jax.ShapeDtypeStruct((DOFS, slots), F32)] * 2,
-        in_specs=[vmem, vmem, hbm, vmem, vmem],
-        out_specs=[hbm] * 2,
-        scratch_shapes=[
-            pltpu.VMEM(extra.shape, F32),
-            pltpu.VMEM((BODY, slots), F32),
-            pltpu.VMEM((BODY, slots), F32),
-            pltpu.SemaphoreType.DMA,
-            pltpu.SemaphoreType.DMA((2 * partners // group,)),
-        ],
-        compiler_params=pltpu.CompilerParams(vmem_limit_bytes=24 * MIB),
-        cost_estimate=pl.CostEstimate(flops=4 * 10**9, bytes_accessed=8 * 10**6, transcendentals=0),
-        name="body_rows",
-    )(recv, flag, extra, off_w, sums_w)
-
-
-def finish_kernel(one, two, rows_of, lanes_of, base, field, step, _, __, fresh, residual, flat):
+    return sends
+
+
+def early_kernel(recv, flag, extra, off_w, sums_w, new, rest, more, sem, *, stop, group):
+    more[...] = jnp.zeros(more.shape, F32)
+    load_overflow(flag, extra, more, sem)
+    slots = group * CAP
+    ready = unpacked(recv, more, slice(0, group))
+    for p in range(0, stop, group):
+        now = ready
+        if p + group < stop:
+            ready = unpacked(recv, more, slice(p + group, p + 2 * group))
+        here = slice(p * CAP, p * CAP + slots)
+        new[:, here], rest[:, here] = body_step(off_w, sums_w, *now)
+
+
+def late_kernel(
+    one, two, rows_of, lanes_of, base, field, step, recv, flag, extra, off_w, sums_w, early, before,
+    fresh, residual, flat, top, bottom, more, new, rest, sem, top_sems, sems, *, start, group,
+):
+    done = [
+        pltpu.make_async_copy(
+            src, dst.at[HEAD:DOFS, 0 : start * CAP], top_sems.at[2 + i]
+        )
+        for i, (src, dst) in enumerate(((early, fresh), (before, residual)))
+    ]
+    for c in done:
+        c.start()
+    more[...] = jnp.zeros(more.shape, F32)
+    load_overflow(flag, extra, more, sem)
     values = jnp.concatenate(
         [one[i : i + 1, :] for i in range(4)] + [two[i : i + 1, :] for i in range(4)], axis=1
     )
@@ -551,31 +552,71 @@
     pieces = jnp.concatenate([spread * hi, spread * mid, spread * low], axis=0)
     found = dot(rows_of[...], pieces, NT)
     flat[...] = found[:, 0:128] + found[:, 128:256] + found[:, 256:384]
-    for b in range(16):
+    blocks = base.shape[1] // 128
+    for b in range(blocks):
         at = slice(b * 128, (b + 1) * 128)
-        added = flat[pl.ds(b, HEAD, stride=16), :]
+        added = flat[pl.ds(b, HEAD, stride=blocks), :]
         scale = step[:, at]
         left = jnp.where(scale > 0.0, base[:, at] - added, 0.0)
-        residual[:, at] = left
-        fresh[:, at] = field[:, at] + scale * left
-
-
-def finish(one, two, rows_of, lanes_of, base, field, step, fresh, residual):
+        bottom[:, at] = left
+        top[:, at] = field[:, at] + scale * left
+    sends = [
+        pltpu.make_async_copy(src, dst.at[0:HEAD, :], top_sems.at[i])
+        for i, (src, dst) in enumerate(((top, fresh), (bottom, residual)))
+    ]
+    for c in sends:
+        c.start()
+    sends += body_blocks(
+        recv, more, off_w, sums_w, fresh, residual, new, rest, sems, start, recv.shape[0], group
+    )
+    for c in done + sends:
+        c.wait()
+
+
+def body_scratch(extra, partners, group):
+    return [
+        pltpu.VMEM(extra.shape, F32),
+        pltpu.VMEM((BODY, partners * CAP), F32),
+        pltpu.VMEM((BODY, partners * CAP), F32),
+        pltpu.SemaphoreType.DMA,
+    ], [pltpu.SemaphoreType.DMA((2 * partners // group,))]
+
+
+def early_rows(recv, flag, extra, off_w, sums_w, stop, group):
     vmem = pl.BlockSpec(memory_space=pltpu.VMEM)
-    there = pl.BlockSpec(memory_space=pl.ANY)
-    first = pl.BlockSpec(base.shape, lambda t: (0, 0))
+    hbm = pl.BlockSpec(memory_space=pltpu.HBM)
     return pl.pallas_call(
-        finish_kernel,
-        grid=(1,),
-        out_shape=[jax.ShapeDtypeStruct(fresh.shape, F32)] * 2,
-        in_specs=[vmem] * 7 + [there] * 2,
-        out_specs=[first] * 2,
-        scratch_shapes=[pltpu.VMEM((HEAD * 16, 128), F32)],
-        input_output_aliases={7: 0, 8: 1},
+        functools.partial(early_kernel, stop=stop, group=group),
+        out_shape=[jax.ShapeDtypeStruct((BODY, stop * CAP), F32)] * 2,
+        in_specs=[vmem, vmem, hbm, vmem, vmem],
+        out_specs=[vmem] * 2,
+        scratch_shapes=[pltpu.VMEM(extra.shape, F32), pltpu.SemaphoreType.DMA],
         compiler_params=pltpu.CompilerParams(vmem_limit_bytes=24 * MIB),
-        cost_estimate=pl.CostEstimate(flops=10**9, bytes_accessed=10**6, transcendentals=0),
-        name="finish",
-    )(one, two, rows_of, lanes_of, base, field, step, fresh, residual)
+        cost_estimate=pl.CostEstimate(flops=4 * 10**9, bytes_accessed=8 * 10**6, transcendentals=0),
+        name="early_rows",
+    )(recv, flag, extra, off_w, sums_w)
+
+
+def late_rows(faces, body, early, before, start, group):
+    recv, _, extra = body[:3]
+    base = faces[4]
+    vmem = pl.BlockSpec(memory_space=pltpu.VMEM)
+    hbm = pl.BlockSpec(memory_space=pltpu.HBM)
+    held, sems = body_scratch(extra, recv.shape[0] - start, group)
+    return pl.pallas_call(
+        functools.partial(late_kernel, start=start, group=group),
+        out_shape=[jax.ShapeDtypeStruct((DOFS, recv.shape[0] * CAP), F32)] * 2,
+        in_specs=[vmem] * 9 + [hbm] + [vmem] * 4,
+        out_specs=[hbm] * 2,
+        scratch_shapes=[pltpu.VMEM((HEAD * 16, 128), F32)]
+        + [pltpu.VMEM(base.shape, F32)] * 2
+        + held
+        + [pltpu.SemaphoreType.DMA((4,))]
+        + sems,
+        compiler_params=pltpu.CompilerParams(vmem_limit_bytes=24 * MIB),
+        cost_estimate=pl.CostEstimate(flops=4 * 10**9, bytes_accessed=8 * 10**6, transcendentals=0),
+        name="late_rows",
+    )(*faces, *body, early, before)
 
 
 def per_device(
@@ -621,8 +662,10 @@
     )
     base, field, step, one, two = head_rows(recv, same, extra, near_w, far_w, face_send, 16)
     one, two = swapped(one, "dev", 0), swapped(two, "dev", 1)
-    fresh, residual = body_rows(recv, same, extra, off_w, sums_w, 32)
-    return tuple(finish(one, two, rows_of, lanes_of, base, field, step, fresh, residual))
+    body = (recv, same, extra, off_w, sums_w)
+    early, before = early_rows(*body, EARLY, 32)
+    faces = (one, two, rows_of, lanes_of, base, field, step)
+    return tuple(late_rows(faces, body, early, before, EARLY, 32))
 
 
 def solution(mesh):

time: 73.8 us -> 73.6 us (level)
  transfers between devices with their start and end apart: 2 -> 2, of which waited for: 0 -> 0; matrix products, arithmetic and copies ran while one was open for 0% -> 0% of each run, Pallas kernels for 7% -> 4%
where the time goes in v5:
time: 73.6 us; the launch traced here: 73.3 us
  blocking collectives  52.9 us (72%)
  Pallas kernels  15.4 us (21%)
  starting transfers between devices  3.3 us (4%)
  between operations  0.76 us (1%)
    all_to_all x1, blocking collectives, exchanged(): lax.all_to_all(rows, ('grp', 'dev'), split_axis=0, concat_axis=0, tiled=T...  52.9 us
    pallas_call x1, Pallas kernels, pack(): pl.pallas_call(pack_kernel, out_shape=[jax.ShapeDtypeStruct((owners, NEAR...  5.84 us
    ppermute x2, starting transfers between devices, swapped(): lax.ppermute(array, axis, [p for i in lower for p in ((i, i + 1), (i + 1,...  3.3 us
    pallas_call x1, Pallas kernels, early_rows(): pl.pallas_call(functools.partial(early_kernel, stop=stop, group=group), o...  3.29 us
    pallas_call x1, Pallas kernels, late_rows(): pl.pallas_call(functools.partial(late_kernel, start=start, group=group),...  2.86 us
    pallas_call x1, Pallas kernels, head_rows(): pl.pallas_call(functools.partial(head_kernel, group=group), out_shape=[ja...  2.64 us
  transfers between devices with their start and end apart: 2, of which 0 were waited for; matrix products, arithmetic and copies ran while one was open for 0% of the time, Pallas kernels for 4%

profile of v5, /device:TPU:1, one launch (start us, length us, event | category | flops | bytes accessed | tf_op | source)
XLA Modules:
  0.0 73.3 jit_solution(14112586087969042828)
XLA Ops:
  0.6 5.8 %pack.1 = (f32[128,48,128]{2,1,0:T(8,128)}, f32[128,8,128]{2,1,0:T(8,128)}, bf16[208,384]{1,0:T(8,128)(2,1)}, bf16[48,384]{1,0:T(8,128)(2,1)}, bf16[400,768]{1,0...) custom-call(s32[1,1024]{1,0:T(1,128)} %bitcast.3, ...), custom_call_target="tpu_custom_call" | custom-call | tf_op jit(solution)/shard_map/pack/pallas_call | solution.py:272
  6.5 52.9 %all_to_all.9.recv = f32[128,48,128]{2,1,0:T(8,128)S(1)} all-to-all(f32[128,48,128]{2,1,0:T(8,128)} %get-tuple-element.30), channel_id=1, replica_groups=mesh['grp'=4,'dev'=32] {'grp','dev'}, dimensions={0} | all-to-all | bytes 6291456 | tf_op jit(solution)/shard_map/all_to_all | solution.py:654
  59.4 0.7 %flag_of.1 = (f32[1,1]{1,0:T(1,128)}, f32[1,1]{1,0:T(1,128)}) custom-call(f32[128,48,128]{2,1,0:T(8,128)S(1)} %all_to_all.9.recv), custom_call_target="tpu_custom_call" | custom-call | tf_op jit(solution)/shard_map/flag_of/pallas_call | solution.py:343
  60.2 0.0 copy-start.3
  60.2 0.0 copy-start.5
  60.2 0.7 while.9
  60.9 0.2 copy-done.3
  61.1 0.0 copy-done.5
  61.1 0.0 copy-done.6
  61.1 0.0 copy-start.7
  61.1 2.6 %head_rows.1 = (f32[24,2048]{1,0:T(8,128)S(1)}, f32[24,2048]{1,0:T(8,128)S(1)}, f32[24,2048]{1,0:T(8,128)S(1)}, f32[4,128]{1,0:T(4,128)S(1)}, f32[4,128]{1,0:T(4,128)S(1)}) custom-call(f32[128,48,128]{2,1,0:T(8,128)S(1)} %all_to_all.9.recv, f32[1,1]{1,0:T(1,128)} %get-tuple-element.31.flag, f32[128,8,128]{2,1,0:T(8,128)} %get-tuple-element.34.extra, ...), custom_call_target="tpu_custom_call" | custom-call | flops 2000000000 | bytes 4000000 | tf_op jit(solution)/shard_map/head_rows/pallas_call | solution.py:426
  63.8 1.4 %collective-permute-start = (f32[4,128]{1,0:T(4,128)S(1)}, f32[4,128]{1,0:T(4,128)S(1)}, u32[]{:S(2)}, u32[]{:S(2)}) collective-permute-start(f32[4,128]{1,0:T(4,128)S(1)} %get-tuple-element.37), channel_id=1, source_target_pairs={{0,1},{1,0},{2,3},{3,2},{4,5},{5,4},{6,7},{7,6},{8,9},{9,8},{10,11... | collective-permute-start | bytes 6152 | tf_op jit(solution)/shard_map/ppermute | solution.py:35
  65.1 1.9 %collective-permute-start.1 = (f32[4,128]{1,0:T(4,128)S(1)}, f32[4,128]{1,0:T(4,128)S(1)}, u32[]{:S(2)}, u32[]{:S(2)}) collective-permute-start(f32[4,128]{1,0:T(4,128)S(1)} %get-tuple-element.38), channel_id=1, source_target_pairs={{1,2},{2,1},{3,4},{4,3},{5,6},{6,5},{7,8},{8,7},{9,10},{10,9},{11,... | collective-permute-start | bytes 6152 | tf_op jit(solution)/shard_map/ppermute | solution.py:35
  67.1 0.0 copy-done.1
  67.1 0.0 copy-done.4
  67.1 0.0 copy-done.7
  67.1 0.0 copy-start
  67.1 0.0 copy-start.2
  67.1 3.3 %early_rows.1 = (f32[192,1536]{1,0:T(8,128)S(1)}, f32[192,1536]{1,0:T(8,128)S(1)}) custom-call(f32[128,48,128]{2,1,0:T(8,128)S(1)} %all_to_all.9.recv, f32[1,1]{1,0:T(1,128)} %get-tuple-element.31.flag, f32[128,8,128]{2,1,0:T(8,128)S(1)} %copy-done.7, bf16[400,768]{1,0:T(8,128)(2,1)S(1)} %copy-done.1, bf16[192,48]{1,0:T(8,128)(2,1)S(1)} %copy-done.4), custom_call_target="tpu_custom_call" | custom-call | flops 4000000000 | bytes 8000000 | tf_op jit(solution)/shard_map/early_rows/pallas_call | solution.py:588
  70.4 0.0 collective-permute-done.one
  70.4 0.0 collective-permute-done.1.two
  70.4 0.0 copy-done
  70.4 0.0 copy-done.2
  70.5 2.9 %late_rows.1 = (f32[216,2048]{1,0:T(8,128)}, f32[216,2048]{1,0:T(8,128)}) custom-call(f32[4,128]{1,0:T(4,128)S(1)} %collective-permute-done.one, f32[4,128]{1,0:T(4,128)S(1)} %collective-permute-done.1.two, bf16[384,1024]{1,0:T(8,128)(2,1)S(1)} %copy-done, bf16[128,1024]{1,0:T(8,128)(2,1)S(1)} %copy-done.2, f32[24,2048]{1,0:T(8,128)S(1)} %get-tuple-element.41.base, ...), custom_call_target="tpu_custom_call" | custom-call | flops 4000000000 | bytes 8000000 | tf_op jit(solution)/shard_map/late_rows/pallas_call | solution.py:606
  (3 shorter events, 0.0 us)
Async XLA Ops:
  60.2 0.9 %copy-start.3 = (bf16[208,384]{1,0:T(8,128)(2,1)S(1)}, bf16[208,384]{1,0:T(8,128)(2,1)}, u32[]{:S(2)}) copy-start(bf16[208,384]{1,0:T(8,128)(2,1)} %get-tuple-element.35.near_w) | copy-start | bytes 479236
  60.2 0.9 %copy-start.5 = (bf16[48,384]{1,0:T(8,128)(2,1)S(1)}, bf16[48,384]{1,0:T(8,128)(2,1)}, u32[]{:S(2)}) copy-start(bf16[48,384]{1,0:T(8,128)(2,1)} %get-tuple-element.36.far_w) | copy-start | bytes 110596
  60.2 0.9 %copy-start.6 = (s32[2,512]{1,0:T(2,128)S(1)}, s32[2,512]{1,0:T(2,128)}, u32[]{:S(2)}) copy-start(s32[2,512]{1,0:T(2,128)} %send.1) | copy-start | bytes 12292
  61.1 6.0 %copy-start.1 = (bf16[400,768]{1,0:T(8,128)(2,1)S(1)}, bf16[400,768]{1,0:T(8,128)(2,1)}, u32[]{:S(2)}) copy-start(bf16[400,768]{1,0:T(8,128)(2,1)} %get-tuple-element.44.off_w) | copy-start | bytes 1843204
  61.1 6.0 %copy-start.4 = (bf16[192,48]{1,0:T(8,128)(2,1)S(1)}, bf16[192,48]{1,0:T(8,128)(2,1)}, u32[]{:S(2)}) copy-start(bf16[192,48]{1,0:T(8,128)(2,1)} %get-tuple-element.45.sums_w) | copy-start | bytes 55300
  61.1 6.0 %copy-start.7 = (f32[128,8,128]{2,1,0:T(8,128)S(1)}, f32[128,8,128]{2,1,0:T(8,128)}, u32[]{:S(2)}) copy-start(f32[128,8,128]{2,1,0:T(8,128)} %get-tuple-element.34.extra) | copy-start | bytes 1572868
  63.8 6.7 %collective-permute-start = (f32[4,128]{1,0:T(4,128)S(1)}, f32[4,128]{1,0:T(4,128)S(1)}, u32[]{:S(2)}, u32[]{:S(2)}) collective-permute-start(f32[4,128]{1,0:T(4,128)S(1)} %get-tuple-element.37), channel_id=1, source_target_pairs={{0,1},{1,0},{2,3},{3,2},{4,5},{5,4},{6,7},{7,6},{8,9},{9,8},{10,11... | collective-permute-start | bytes 6152 | tf_op jit(solution)/shard_map/ppermute | solution.py:35
  65.1 5.3 %collective-permute-start.1 = (f32[4,128]{1,0:T(4,128)S(1)}, f32[4,128]{1,0:T(4,128)S(1)}, u32[]{:S(2)}, u32[]{:S(2)}) collective-permute-start(f32[4,128]{1,0:T(4,128)S(1)} %get-tuple-element.38), channel_id=1, source_target_pairs={{1,2},{2,1},{3,4},{4,3},{5,6},{6,5},{7,8},{8,7},{9,10},{10,9},{11,... | collective-permute-start | bytes 6152 | tf_op jit(solution)/shard_map/ppermute | solution.py:35
  67.1 3.3 %copy-start = (bf16[384,1024]{1,0:T(8,128)(2,1)S(1)}, bf16[384,1024]{1,0:T(8,128)(2,1)}, u32[]{:S(2)}) copy-start(bf16[384,1024]{1,0:T(8,128)(2,1)} %get-tuple-element.39.rows_of) | copy-start | bytes 2359300
  67.1 3.3 %copy-start.2 = (bf16[128,1024]{1,0:T(8,128)(2,1)S(1)}, bf16[128,1024]{1,0:T(8,128)(2,1)}, u32[]{:S(2)}) copy-start(bf16[128,1024]{1,0:T(8,128)(2,1)} %get-tuple-element.40.lanes_of) | copy-start | bytes 786436
